TPU v7x, 256 devices: a whole 4x4x8 slice. The times are simulated.
256 devices in a mesh: dp: 8 (over y_hi, x), pencil: 32 (over z, y_lo, core).
Axes of the slice: x: 4, y: 4 (y_hi: 2, y_lo: 2; y = y_hi * 2 + y_lo), z: 8, core: 2. Of those that a mesh axis runs over, the one named last changes fastest.
Arguments:
- field_in: bfloat16 [8, 128, 48, 8192], P('dp', 'pencil'), may hold values from -6 to 6
- grad_out: bfloat16 [8, 128, 48, 8192], P('dp', 'pencil'), may hold values from -6 to 6
- w_spec: float32 [2, 32, 16, 32, 2304], P(None, 'pencil', 'dp'), may hold values from -6 to 6
- w_local: bfloat16 [48, 48], replicated, may hold values from -0.875 to 0.875
Outputs:
- grad_in: bfloat16 [8, 128, 48, 8192], P('dp', 'pencil')
- grad_spec: float32 [2, 32, 16, 32, 2304], P(None, 'pencil', 'dp')
- grad_local: float32 [48, 48], replicated
All inputs are finite; a program needn't handle non-finite values.
Results may differ from a plain program's by a relative error of at most 0.009.
Values sent between devices are 32-bit elements; how exact they have to be, the bound alone decides.
A program may use at most 192 MiB of HBM per device.

v0:
```python
import functools

import jax
import jax.numpy as jnp
import ml_dtypes
import numpy as np
from jax import lax
from jax.experimental import pallas as pl
from jax.experimental.pallas import tpu as pltpu
from jax.sharding import PartitionSpec as P

X = 128
Y = 128
Z = 64
C = 48
KX = 32
KY = 32
KZ = 16
ROWS = 4
GROUP = 4
LANES = 128
LIMIT = 56 * 1024 * 1024

MESH = pl.DeviceIdType.MESH
f32 = jnp.float32
bf16 = jnp.bfloat16


def split(table):
    high = table.astype(np.float32).astype(ml_dtypes.bfloat16)
    low = (table - high.astype(np.float64)).astype(np.float32).astype(ml_dtypes.bfloat16)
    return high, low


def signed(count):
    freqs = np.arange(count)
    return np.where(freqs < count // 2, freqs, freqs - count)


def forward_table(length, count):
    angles = 2.0 * np.pi * (np.outer(signed(count), np.arange(length)) % length) / length
    cos, sin = np.cos(angles), np.sin(angles)
    table = np.zeros((2, count, length, 2))
    table[0, :, :, 0] = cos
    table[0, :, :, 1] = sin
    table[1, :, :, 0] = -sin
    table[1, :, :, 1] = cos
    return table.reshape(2 * count, length, 2)


def z_table(scale):
    angles = 2.0 * np.pi * (np.outer(np.arange(KZ), np.arange(Z)) % Z) / Z
    table = np.zeros((KZ, GROUP, 2, GROUP, Z))
    for place in range(GROUP):
        table[:, place, 0, place] = np.cos(angles) * scale[:, None]
        table[:, place, 1, place] = -np.sin(angles) * scale[:, None]
    return table.reshape(KZ * GROUP * 2, GROUP * Z)


def z_scale():
    return np.where(np.arange(KZ) == 0, 1.0, 2.0) / float(X * Y * Z)


def tall(table):
    return np.concatenate(split(table), axis=0)


def wide3(table):
    high, low = split(table)
    return np.concatenate([high, low, high], axis=1)


def y_forward():
    return forward_table(Y, KY).reshape(2 * KY, Y * 2)


def x_forward():
    table = forward_table(X, KX).reshape(2 * KX, X // ROWS, ROWS, 2)
    return table.transpose(0, 1, 3, 2).reshape(2 * KX, X * 2)


def nt(left, right):
    return lax.dot_general(left, right, (((1,), (1,)), ((), ())), preferred_element_type=f32)


def tn(left, right):
    return lax.dot_general(left, right, (((0,), (0,)), ((), ())), preferred_element_type=f32)


def nn(left, right):
    return jnp.dot(left, right, preferred_element_type=f32)


def halves(values):
    high = values.astype(bf16)
    low = (values - high.astype(f32)).astype(bf16)
    return high, low


def cells(ref, block):
    return ref[:, :, pl.ds(pl.multiple_of(block * GROUP * Z, GROUP * Z), GROUP * Z)].reshape(
        ROWS * C, GROUP * Z
    )


def z_forward(values, table, q_ref, block):
    both = nt(table, values)
    half = KZ * GROUP * 2
    part = both[:half] + both[half:]
    q_ref[:, pl.ds(pl.multiple_of(block * 8, 8), 8), :] = part.reshape(KZ, 8, ROWS * C)


def y_to_message(q_ref, dy_ref, o_ref, msg_ref):
    table = dy_ref[...]
    for kz in range(KZ):
        both = nn(table, q_ref[kz].astype(bf16))
        o_ref[kz] = both[: 2 * KY] + both[2 * KY :]
    for ri in range(2):
        for x in range(ROWS):
            row = jnp.concatenate(
                [
                    o_ref[kz, ri * KY : (ri + 1) * KY, x * C : (x + 1) * C]
                    for kz in range(KZ)
                ],
                axis=1,
            )
            for t in range(KZ * C // LANES):
                msg_ref[t, pl.ds(ri * ROWS + x, KY, stride=8), :] = row[
                    :, t * LANES : (t + 1) * LANES
                ]


def message_to_y(rb_ref, ey_ref, b_ref, q_ref):
    b_ref[...] = jnp.zeros_like(b_ref)
    for ri in range(2):
        for x in range(ROWS):
            row = jnp.concatenate(
                [
                    rb_ref[t, pl.ds(ri * ROWS + x, KY, stride=8), :]
                    for t in range(KZ * C // LANES)
                ],
                axis=1,
            )
            for kz in range(KZ):
                b_ref[kz, ri * KY : (ri + 1) * KY, x * C : (x + 1) * C] = row[
                    :, kz * C : (kz + 1) * C
                ]
    table = ey_ref[...]
    for kz in range(KZ):
        high, low = halves(b_ref[kz])
        q_ref[kz] = nn(table, jnp.concatenate([high, high, low], axis=0))


def z_backward(q_ref, table, block):
    part = q_ref[:, pl.ds(pl.multiple_of(block * 8, 8), 8), :]
    part = part.reshape(KZ * 8, q_ref.shape[2])
    turned = part.T[: ROWS * C].astype(bf16)
    return nn(jnp.concatenate([turned, turned], axis=1), table)


def gelu_slope(values):
    size = jnp.abs(values)
    bell = jnp.exp(values * values * -0.5)
    t = 1.0 / (1.0 + (0.3275911 * 0.7071067811865476) * size)
    poly = 0.5 * 1.061405429
    poly = poly * t + 0.5 * -1.453152027
    poly = poly * t + 0.5 * 1.421413741
    poly = poly * t + 0.5 * -0.284496736
    poly = poly * t + 0.5 * 0.254829592
    tail = poly * t * bell
    cumul = jnp.where(values >= 0.0, 1.0 - tail, tail)
    return cumul + values * bell * 0.3989422804014327


def first_kernel(x_ref, bdz_ref, dy_ref, msg_ref, q_ref, o_ref):
    table = bdz_ref[...]

    def step(block, carry):
        z_forward(cells(x_ref, block), table, q_ref, block)
        return carry

    lax.fori_loop(0, Y // GROUP, step, 0, unroll=4)
    y_to_message(q_ref, dy_ref, o_ref, msg_ref)


def middle_kernel(
    rb_ref, x_ref, go_ref, wl_ref, ey_ref, bdzs_ref, bdzg_ref, dy_ref,
    s_ref, msg_ref, gl_ref, b_ref, q2_ref, q_ref, o_ref, acc_ref,
):
    message_to_y(rb_ref, ey_ref, b_ref, q2_ref)
    synth = bdzs_ref[...]
    table = bdzg_ref[...]
    mixing = wl_ref[...]
    acc_ref[...] = jnp.zeros_like(acc_ref)

    def step(block, carry):
        values = cells(x_ref, block)
        preact = z_backward(q2_ref, synth, block) + nn(mixing, values)
        slopes = cells(go_ref, block).astype(f32) * gelu_slope(preact)
        half = slopes.astype(bf16)
        s_ref[:, :, pl.ds(pl.multiple_of(block * GROUP * Z, GROUP * Z), GROUP * Z)] = half.reshape(
            ROWS, C, GROUP * Z
        )
        z_forward(half, table, q_ref, block)
        acc_ref[...] += nt(values, half)
        return carry

    lax.fori_loop(0, Y // GROUP, step, 0)
    gl_ref[...] = jnp.zeros_like(gl_ref)
    total = acc_ref[0:C, 0:C]
    for x in range(1, ROWS):
        total = total + acc_ref[x * C : (x + 1) * C, x * C : (x + 1) * C]
    gl_ref[:, :, 0:C] = total.reshape(C // 8, 8, C)
    y_to_message(q_ref, dy_ref, o_ref, msg_ref)


def last_kernel(rb_ref, s_ref, wl_ref, ey_ref, bdzs_ref, out_ref, b_ref, q2_ref):
    message_to_y(rb_ref, ey_ref, b_ref, q2_ref)
    synth = bdzs_ref[...]
    mixing = wl_ref[...]

    def step(block, carry):
        values = cells(s_ref, block)
        total = z_backward(q2_ref, synth, block) + nn(mixing, values)
        out_ref[:, :, pl.ds(pl.multiple_of(block * GROUP * Z, GROUP * Z), GROUP * Z)] = (
            total.astype(bf16).reshape(ROWS, C, GROUP * Z)
        )
        return carry

    lax.fori_loop(0, Y // GROUP, step, 0, unroll=2)


def others(axis, count, body):
    me = lax.axis_index(axis)

    def step(k, carry):
        body(lax.rem(me + k, count))
        return carry

    lax.fori_loop(1, count, step, 0)


def enter(n, d):
    barrier = pltpu.get_barrier_semaphore()
    for axis, count in (("pencil", n), ("dp", d)):
        others(
            axis,
            count,
            lambda j, axis=axis: pl.semaphore_signal(
                barrier, inc=1, device_id={axis: j}, device_id_type=MESH
            ),
        )
    return barrier


def remote(src, dst, sems, kind, mine, axis, j):
    return pltpu.make_async_remote_copy(
        src_ref=src,
        dst_ref=dst,
        send_sem=sems.at[2 * kind, j],
        recv_sem=sems.at[2 * kind + 1, mine],
        device_id={axis: j},
        device_id_type=MESH,
    )


def waits(view, sems, kind, axis, count):
    def one(j):
        copy = pltpu.make_async_copy(view(j), view(j), sems.at[2 * kind + 1, j])
        copy.wait()

    others(axis, count, one)


def sent(view, sems, kind, axis, count):
    def one(j):
        copy = pltpu.make_async_copy(view(j), view(j), sems.at[2 * kind, j])
        copy.wait()

    others(axis, count, one)


def rows8(ref):
    return lambda j: ref.at[:, pl.ds(pl.multiple_of(j * 8, 8), 8), :]


def modes(ref):
    return lambda j: ref.at[pl.ds(pl.multiple_of(j * 2 * KX, 2 * KX), 2 * KX), :]


def swap(src, dst, sems, kind, axis, count):
    me = lax.axis_index(axis)
    others(axis, count, lambda j: remote(src(j), dst(me), sems, kind, me, axis, j).start())


def x_analyse(r_ref, dx_ref, g_ref, d):
    high, low = halves(jnp.concatenate([r_ref[t] for t in range(r_ref.shape[0])], axis=1))
    table = dx_ref[...]
    both = nn(table, high)
    spectrum = both[: 2 * KX] + both[2 * KX :] + nn(table[: 2 * KX], low)
    width = KZ * C // d
    pad = jnp.zeros((2 * KX, LANES - width), f32)
    for j in range(d):
        g_ref[j * 2 * KX : (j + 1) * 2 * KX, :] = jnp.concatenate(
            [spectrum[:, j * width : (j + 1) * width], pad], axis=1
        )


def x_synth(h_ref, ex_ref, mb_ref, d):
    width = KZ * C // d
    spectrum = jnp.concatenate(
        [h_ref[j * 2 * KX : (j + 1) * 2 * KX, 0:width] for j in range(d)], axis=1
    )
    high, low = halves(spectrum)
    rows = nn(ex_ref[...], jnp.concatenate([high, high, low], axis=0))
    for t in range(mb_ref.shape[0]):
        mb_ref[t] = rows[:, t * LANES : (t + 1) * LANES]


def pick(ref, kx, d):
    real = ref[pl.ds(kx, d, stride=2 * KX), :]
    imag = ref[pl.ds(KX + kx, d, stride=2 * KX), :]
    return real, imag


def forward_mix_kernel(
    n, d, msg_ref, dx_ref, ex_ref, wc_ref,
    rb_out, h_out,
    r_ref, g_ref, h_ref, g2_ref, h2_ref, mb_ref, rb_ref, psem, dsem,
):
    me, sample = lax.axis_index("pencil"), lax.axis_index("dp")
    barrier = enter(n, d)
    pl.semaphore_wait(barrier, n + d - 2)
    swap(rows8(msg_ref), rows8(r_ref), psem, 0, "pencil", n)
    mine = pl.ds(pl.multiple_of(me * 8, 8), 8)
    r_ref[:, mine, :] = msg_ref[:, mine, :]
    waits(rows8(r_ref), psem, 0, "pencil", n)
    x_analyse(r_ref, dx_ref, g_ref, d)
    own = pl.ds(pl.multiple_of(sample * 2 * KX, 2 * KX), 2 * KX)
    swap(modes(g_ref), modes(h_ref), dsem, 0, "dp", d)
    h_ref[own, :] = g_ref[own, :]
    waits(modes(h_ref), dsem, 0, "dp", d)

    def mix(kx, carry):
        real, imag = pick(h_ref, kx, d)
        high, low = halves(jnp.concatenate([real, imag], axis=0))
        left = jnp.concatenate(
            [
                jnp.concatenate([high, high], axis=1),
                jnp.concatenate([low, jnp.zeros_like(low)], axis=1),
            ],
            axis=0,
        )
        both = nn(left, wc_ref[kx])
        both = both[: 2 * d] + both[2 * d :]
        g2_ref[pl.ds(kx, d, stride=2 * KX), :] = both[:d, :LANES] - both[d:, LANES:]
        g2_ref[pl.ds(KX + kx, d, stride=2 * KX), :] = both[:d, LANES:] + both[d:, :LANES]
        return carry

    lax.fori_loop(0, KX, mix, 0, unroll=4)
    swap(modes(g2_ref), modes(h2_ref), dsem, 1, "dp", d)
    h2_ref[own, :] = g2_ref[own, :]
    h_out[...] = h_ref[...]
    waits(modes(h2_ref), dsem, 1, "dp", d)
    x_synth(h2_ref, ex_ref, mb_ref, d)
    swap(rows8(mb_ref), rows8(rb_ref), psem, 1, "pencil", n)
    rb_ref[:, mine, :] = mb_ref[:, mine, :]
    sent(rows8(msg_ref), psem, 0, "pencil", n)
    sent(modes(g_ref), dsem, 0, "dp", d)
    sent(modes(g2_ref), dsem, 1, "dp", d)
    waits(rows8(rb_ref), psem, 1, "pencil", n)
    rb_out[...] = rb_ref[...]
    sent(rows8(mb_ref), psem, 1, "pencil", n)


def backward_mix_kernel(
    n, d, msg_ref, dx_ref, ex_ref, wc_ref, si_ref, gl_ref,
    rb_out, gs_out, gl_out,
    r_ref, g_ref, h_ref, g2_ref, h2_ref, mb_ref, rb_ref,
    glr_ref, glp_ref, gld_ref, glt_ref, glf_ref, psem, dsem, qsem, esem,
):
    me, sample = lax.axis_index("pencil"), lax.axis_index("dp")
    tiles = C // 8
    keeper = me < tiles
    barrier = enter(n, d)
    pl.semaphore_wait(barrier, n + d - 2)
    swap(rows8(msg_ref), rows8(r_ref), psem, 0, "pencil", n)

    def to_keeper(j):
        @pl.when(j < tiles)
        def _():
            remote(gl_ref.at[j], glr_ref.at[me], qsem, 0, me, "pencil", j).start()

    others("pencil", n, to_keeper)
    mine = pl.ds(pl.multiple_of(me * 8, 8), 8)
    r_ref[:, mine, :] = msg_ref[:, mine, :]

    @pl.when(keeper)
    def _():
        glr_ref[me] = gl_ref[me]

    waits(rows8(r_ref), psem, 0, "pencil", n)
    x_analyse(r_ref, dx_ref, g_ref, d)
    own = pl.ds(pl.multiple_of(sample * 2 * KX, 2 * KX), 2 * KX)
    swap(modes(g_ref), modes(h_ref), dsem, 0, "dp", d)

    @pl.when(keeper)
    def _():
        waits(lambda j: glr_ref.at[j], qsem, 0, "pencil", n)
        glp_ref[...] = jnp.sum(glr_ref[...], axis=0)
        others(
            "dp",
            d,
            lambda j: remote(glp_ref, gld_ref.at[sample], esem, 0, sample, "dp", j).start(),
        )
        gld_ref[sample] = glp_ref[...]

    h_ref[own, :] = g_ref[own, :]
    waits(modes(h_ref), dsem, 0, "dp", d)

    def stacked(kx):
        real, imag = pick(h_ref, kx, d)
        return halves(
            jnp.concatenate(
                [
                    jnp.concatenate([real, imag], axis=1),
                    jnp.concatenate([imag, -real], axis=1),
                ],
                axis=0,
            )
        )

    def adjoint(kx, carry):
        high, low = stacked(kx)
        both = nt(jnp.concatenate([high, low], axis=0), wc_ref[kx])
        total = both[: 2 * d, :LANES] + both[: 2 * d, LANES:] + both[2 * d :, :LANES]
        g2_ref[pl.ds(kx, d, stride=2 * KX), :] = total[:d]
        g2_ref[pl.ds(KX + kx, d, stride=2 * KX), :] = total[d:]
        return carry

    lax.fori_loop(0, KX, adjoint, 0, unroll=4)
    swap(modes(g2_ref), modes(h2_ref), dsem, 1, "dp", d)
    h2_ref[own, :] = g2_ref[own, :]
    waits(modes(h2_ref), dsem, 1, "dp", d)
    x_synth(h2_ref, ex_ref, mb_ref, d)
    swap(rows8(mb_ref), rows8(rb_ref), psem, 1, "pencil", n)
    rb_ref[:, mine, :] = mb_ref[:, mine, :]

    @pl.when(keeper)
    def _():
        waits(lambda j: gld_ref.at[j], esem, 0, "dp", d)
        glt_ref[...] = jnp.sum(gld_ref[...], axis=0)
        others(
            "pencil",
            n,
            lambda j: remote(glt_ref, glf_ref.at[me], qsem, 1, me, "pencil", j).start(),
        )
        glf_ref[me] = glt_ref[...]

    def weight_grad(kx, carry):
        high, low = stacked(kx)
        real, imag = pick(si_ref, kx, d)
        shigh, slow = halves(jnp.concatenate([real, imag], axis=0))
        product = tn(
            jnp.concatenate([shigh, slow, shigh], axis=0),
            jnp.concatenate([high, high, low], axis=0),
        )
        for ri in range(2):
            for kz in range(2):
                gs_out[ri, kz, kx] = product[
                    kz * C : (kz + 1) * C, ri * LANES + kz * C : ri * LANES + (kz + 1) * C
                ]
        return carry

    lax.fori_loop(0, KX, weight_grad, 0, unroll=2)
    sent(rows8(msg_ref), psem, 0, "pencil", n)
    sent(modes(g_ref), dsem, 0, "dp", d)
    sent(modes(g2_ref), dsem, 1, "dp", d)

    def keeper_sent(j):
        @pl.when(j < tiles)
        def _():
            pltpu.make_async_copy(gl_ref.at[j], gl_ref.at[j], qsem.at[0, j]).wait()

    others("pencil", n, keeper_sent)

    def tile_arrived(j):
        @pl.when(j < tiles)
        def _():
            pltpu.make_async_copy(glf_ref.at[j], glf_ref.at[j], qsem.at[3, j]).wait()

    others("pencil", n, tile_arrived)
    gl_out[...] = glf_ref[...]

    @pl.when(keeper)
    def _():
        sent(lambda j: glp_ref, esem, 0, "dp", d)
        sent(lambda j: glt_ref, qsem, 1, "pencil", n)

    waits(rows8(rb_ref), psem, 1, "pencil", n)
    rb_out[...] = rb_ref[...]
    sent(rows8(mb_ref), psem, 1, "pencil", n)


def vmem(count):
    return [pl.BlockSpec(memory_space=pltpu.VMEM)] * count


def call(body, shapes, scratch, arguments, name, collective=None, flops=1_000_000_000):
    extra = {}
    if collective is not None:
        extra = {"collective_id": collective, "has_side_effects": True}
    return pl.pallas_call(
        body,
        out_shape=shapes,
        in_specs=vmem(len(arguments)),
        out_specs=jax.tree.map(lambda _: pl.BlockSpec(memory_space=pltpu.VMEM), shapes),
        scratch_shapes=scratch,
        compiler_params=pltpu.CompilerParams(vmem_limit_bytes=LIMIT, **extra),
        cost_estimate=pl.CostEstimate(flops=flops, bytes_accessed=4_000_000, transcendentals=0),
        name=name,
    )(*arguments)


def stage_weights(w_spec):
    shaped = w_spec.reshape(2, 2, KX, C, C)
    high = lax.reduce_precision(shaped, 8, 7)
    parts = jnp.stack([high, shaped - high]).astype(bf16)
    pad = LANES - 2 * C
    first = jnp.pad(parts[:, :, 0], ((0, 0), (0, 0), (0, 0), (0, C + pad), (0, C + pad)))
    second = jnp.pad(parts[:, :, 1], ((0, 0), (0, 0), (0, 0), (C, pad), (C, pad)))
    both = first + second
    return both.transpose(2, 0, 3, 1, 4).reshape(KX, 2 * LANES, 2 * LANES)


def local(n, d, field_in, grad_out, w_spec, w_local):
    sds = jax.ShapeDtypeStruct
    tiles = KZ * C // LANES
    values, upstream = field_in[0], grad_out[0]
    cells_shape = values.shape
    ones = np.ones((KZ,))
    scale = z_scale()
    bdz = tall(z_table(ones))
    bdz_grad = tall(z_table(scale))
    synth = tall(z_table(scale))
    synth_plain = tall(z_table(ones))
    dy = tall(y_forward())
    ey = wide3(y_forward().T)
    dx = tall(x_forward())
    ex = wide3(x_forward().T)
    eye = jnp.eye(ROWS, dtype=bf16)
    mixing_back = jnp.kron(eye, w_local)
    mixing = jnp.kron(eye, w_local.T)
    weights = stage_weights(w_spec)

    message = sds((tiles, n * 8, LANES), f32)
    q_shape = pltpu.VMEM((KZ, Y * 2, ROWS * C), f32)
    q2_shape = pltpu.VMEM((KZ, Y * 2, 2 * LANES), f32)
    o_shape = pltpu.VMEM((KZ, 2 * KY, ROWS * C), f32)
    b_shape = pltpu.VMEM((KZ, 2 * KY, 2 * LANES), f32)
    mode_shape = pltpu.VMEM((d * 2 * KX, LANES), f32)
    message_shape = pltpu.VMEM((tiles, n * 8, LANES), f32)
    exchange = [message_shape] + [mode_shape] * 4 + [message_shape] * 2

    msg = call(first_kernel, message, [q_shape, o_shape], (values, bdz, dy), "plane_analysis")
    rb, spec_in = call(
        functools.partial(forward_mix_kernel, n, d),
        (message, sds((d * 2 * KX, LANES), f32)),
        exchange + [pltpu.SemaphoreType.DMA((4, n)), pltpu.SemaphoreType.DMA((4, d))],
        (msg, dx, ex, weights),
        "forward_modes",
        collective=0,
    )
    slopes, msg, local_terms = call(
        middle_kernel,
        (sds(cells_shape, bf16), message, sds((C // 8, 8, LANES), f32)),
        [b_shape, q2_shape, q_shape, o_shape, pltpu.VMEM((ROWS * C, ROWS * C), f32)],
        (rb, values, upstream, mixing, ey, synth, bdz_grad, dy),
        "slopes_and_analysis",
    )
    tile = pltpu.VMEM((8, LANES), f32)
    rb, grad_modes, grad_local = call(
        functools.partial(backward_mix_kernel, n, d),
        (message, sds((2, 2, KX, C, C), f32), sds((C // 8, 8, LANES), f32)),
        exchange
        + [
            pltpu.VMEM((n, 8, LANES), f32),
            tile,
            pltpu.VMEM((d, 8, LANES), f32),
            tile,
            pltpu.VMEM((C // 8, 8, LANES), f32),
            pltpu.SemaphoreType.DMA((4, n)),
            pltpu.SemaphoreType.DMA((4, d)),
            pltpu.SemaphoreType.DMA((4, n)),
            pltpu.SemaphoreType.DMA((2, d)),
        ],
        (msg, dx, ex, weights, spec_in, local_terms),
        "backward_modes",
        collective=1,
    )
    grad_in = call(
        last_kernel,
        sds(cells_shape, bf16),
        [b_shape, q2_shape],
        (rb, slopes, mixing_back, ey, synth_plain),
        "plane_synthesis",
    )
    grad_spec = grad_modes.reshape(2, 1, 2, KX, C * C)
    return grad_in[None], grad_spec, grad_local.reshape(C, LANES)[:, :C]


def solution(mesh):
    n, d = mesh.shape["pencil"], mesh.shape["dp"]
    placed = (
        P("dp", "pencil", None, None),
        P("dp", "pencil", None, None),
        P(None, "pencil", "dp", None, None),
        P(),
    )
    return jax.shard_map(
        functools.partial(local, n, d),
        mesh=mesh,
        in_specs=placed,
        out_specs=(P("dp", "pencil", None, None), P(None, "pencil", "dp", None, None), P()),
        check_vma=False,
    )
```

profile of v0, /device:TPU:1, one launch (start us, length us, event | category | flops | bytes accessed | tf_op | source)
XLA Modules:
  0.0 203.8 jit_solution(4055200796541304130)
XLA Ops:
  0.6 0.8 copy.21
  1.4 0.9 broadcast_multiply_fusion
  2.4 0.8 mul.47.wl_ref
  3.1 0.8 mul.44.wl_ref
  3.9 6.3 %plane_analysis.1.msg_ref = f32[6,256,128]{2,1,0:T(8,128)} custom-call(bf16[4,48,8192]{2,1,0:T(8,128)(2,1)} %bitcast.19, bf16[256,256]{1,0:T(8,128)(2,1)} %constant.15.clone.bdz_ref.bdzs_ref, bf16[128,256]{1,0:T(8,128)(2,1)} %constant.16.clone.dy_ref), custom_call_target="tpu_custom_call" | custom-call | flops 1000000000 | bytes 4000000 | tf_op jit(solution)/shard_map/plane_analysis/pallas_call | solution.py:513
  10.3 3.1 %reshape.60 = f32[1,2,2,32,48,48]{5,4,3,2,1,0:T(8,128)S(1)} reshape(f32[2,1,2,32,2304]{4,3,2,1,0:T(8,128)} %param.14) | data formatting | bytes 2359296 | tf_op jit(solution)/shard_map/reshape | solution.py:526
  13.3 0.5 reduce-precision_convert_fusion
  13.9 0.7 fusion.2
  14.5 1.2 add_bitcast_fusion
  15.7 6.4 %copy.20 = bf16[32,2,128,2,128]{4,3,2,1,0:T(2,128)(2,1)} copy(bf16[32,2,128,2,128]{4,2,0,3,1:T(8,128)(2,1)S(1)} %add_bitcast_fusion) | data formatting | bytes 8388608 | tf_op jit(solution)/shard_map/transpose | solution.py:533
  22.1 7.6 %reshape.61.wc_ref = bf16[32,256,256]{2,1,0:T(8,128)(2,1)} reshape(bf16[32,2,128,2,128]{4,3,2,1,0:T(2,128)(2,1)} %copy.20) | data formatting | bytes 8388608 | tf_op jit(solution)/shard_map/reshape | solution.py:533
  29.7 69.6 %forward_modes.1 = (f32[6,256,128]{2,1,0:T(8,128)}, f32[512,128]{1,0:T(8,128)}) custom-call(f32[6,256,128]{2,1,0:T(8,128)} %plane_analysis.1.msg_ref, bf16[128,256]{1,0:T(8,128)(2,1)} %constant.17.clone.dx_ref, bf16[256,192]{1,0:T(8,128)(2,1)} %constant.18.clone.ex_ref, bf16[32,256,256]{2,1,0:T(8,128)(2,1)} %reshape.61.wc_ref), custom_call_target="tpu_custom_call" | custom-call | flops 1000000000 | bytes 4000000 | tf_op jit(solution)/shard_map/forward_modes/pallas_call | solution.py:513
  99.3 25.5 %slopes_and_analysis.1 = (bf16[4,48,8192]{2,1,0:T(8,128)(2,1)}, f32[6,256,128]{2,1,0:T(8,128)}, f32[6,8,128]{2,1,0:T(8,128)}) custom-call(f32[6,256,128]{2,1,0:T(8,128)} %get-tuple-element.11.rb_ref, bf16[4,48,8192]{2,1,0:T(8,128)(2,1)} %bitcast.20, bf16[4,48,8192]{2,1,0:T(8,128)(2,1)} %bitcast.22, bf16[192,192]{1,0:T(8,128)(2,1)} %mul.44.wl_ref, ...), custom_call_target="tpu_custom_call" | custom-call | flops 1000000000 | bytes 4000000 | tf_op jit(solution)/shard_map/slopes_and_analysis/pallas_call | solution.py:513
  124.8 66.6 %backward_modes.1 = (f32[6,256,128]{2,1,0:T(8,128)}, f32[2,2,32,48,48]{4,3,2,1,0:T(8,128)}, f32[6,8,128]{2,1,0:T(8,128)}) custom-call(f32[6,256,128]{2,1,0:T(8,128)} %get-tuple-element.12.msg_ref, bf16[128,256]{1,0:T(8,128)(2,1)} %constant.17.clone.dx_ref, bf16[256,192]{1,0:T(8,128)(2,1)} %constant.18.clone.ex_ref, bf16[32,256,256]{2,1,0:T(8,128)(2,1)} %reshape.61.wc_ref, ...), custom_call_target="tpu_custom_call" | custom-call | flops 1000000000 | bytes 4000000 | tf_op jit(solution)/shard_map/backward_modes/pallas_call | solution.py:513
  191.3 0.0 copy-start
  191.4 9.7 %plane_synthesis.1 = bf16[4,48,8192]{2,1,0:T(8,128)(2,1)} custom-call(f32[6,256,128]{2,1,0:T(8,128)} %get-tuple-element.15.rb_ref, bf16[4,48,8192]{2,1,0:T(8,128)(2,1)} %get-tuple-element.16.s_ref, bf16[192,192]{1,0:T(8,128)(2,1)} %mul.47.wl_ref, bf16[256,192]{1,0:T(8,128)(2,1)} %constant.19.clone.ey_ref, bf16[256,256]{1,0:T(8,128)(2,1)} %constant.15.clone.bdz_ref.bdzs_ref), custom_call_target="tpu_custom_call" | custom-call | flops 1000000000 | bytes 4000000 | tf_op jit(solution)/shard_map/plane_synthesis/pallas_call | solution.py:513
  201.0 0.0 copy-start.1
  201.0 0.0 copy-done
  201.0 2.2 %reshape.62 = f32[2,1,2,32,2304]{4,3,2,0,1:T(8,128)} reshape(f32[2,2,32,48,48]{4,3,2,1,0:T(8,128)S(1)} %copy-done) | data formatting | bytes 2359296 | tf_op jit(solution)/shard_map/reshape | solution.py:608
  203.2 0.0 copy-done.1
  203.2 0.6 copy.25
  (1 shorter events, 0.0 us)
Async XLA Ops:
  191.3 9.7 %copy-start = (f32[2,2,32,48,48]{4,3,2,1,0:T(8,128)S(1)}, f32[2,2,32,48,48]{4,3,2,1,0:T(8,128)}, u32[]{:S(2)}) copy-start(f32[2,2,32,48,48]{4,3,2,1,0:T(8,128)} %get-tuple-element.17) | copy-start | bytes 3538948
  201.0 2.2 %copy-start.1 = (f32[6,8,128]{2,1,0:T(8,128)S(1)}, f32[6,8,128]{2,1,0:T(8,128)}, u32[]{:S(2)}) copy-start(f32[6,8,128]{2,1,0:T(8,128)} %get-tuple-element.18) | copy-start | bytes 73732
where the time goes:
time: 204 us
  Pallas kernels  178 us (87%)
  local copies, waits for them, and re-layouts  22.2 us (11%)
  other arithmetic  3.31 us (2%)
    pallas_call x5, Pallas kernels, call(): pl.pallas_call(body, out_shape=shapes, in_specs=vmem(len(arguments)), out...  178 us
    reshape x1, local copies, waits for them, and re-layouts, stage_weights(): return both.transpose(2, 0, 3, 1, 4).reshape(KX, 2 * LANES, 2 * LANES)  7.57 us
    transpose x1, local copies, waits for them, and re-layouts, stage_weights(): return both.transpose(2, 0, 3, 1, 4).reshape(KX, 2 * LANES, 2 * LANES)  6.36 us

commit v1 on v0

v1 whole, which is shorter than its diff:
```python
import functools

import jax
import jax.numpy as jnp
import ml_dtypes
import numpy as np
from jax import lax
from jax.experimental import pallas as pl
from jax.experimental.pallas import tpu as pltpu
from jax.sharding import PartitionSpec as P

X = 128
Y = 128
Z = 64
C = 48
KX = 32
KY = 32
KZ = 16
ROWS = 4
GROUP = 4
LANES = 128
LIMIT = 56 * 1024 * 1024

MESH = pl.DeviceIdType.MESH
f32 = jnp.float32
bf16 = jnp.bfloat16


def split(table):
    high = table.astype(np.float32).astype(ml_dtypes.bfloat16)
    low = (table - high.astype(np.float64)).astype(np.float32).astype(ml_dtypes.bfloat16)
    return high, low


def signed(count):
    freqs = np.arange(count)
    return np.where(freqs < count // 2, freqs, freqs - count)


def forward_table(length, count):
    angles = 2.0 * np.pi * (np.outer(signed(count), np.arange(length)) % length) / length
    cos, sin = np.cos(angles), np.sin(angles)
    table = np.zeros((2, count, length, 2))
    table[0, :, :, 0] = cos
    table[0, :, :, 1] = sin
    table[1, :, :, 0] = -sin
    table[1, :, :, 1] = cos
    return table.reshape(2 * count, length, 2)


def z_table(scale):
    angles = 2.0 * np.pi * (np.outer(np.arange(KZ), np.arange(Z)) % Z) / Z
    table = np.zeros((KZ, GROUP, 2, GROUP, Z))
    for place in range(GROUP):
        table[:, place, 0, place] = np.cos(angles) * scale[:, None]
        table[:, place, 1, place] = -np.sin(angles) * scale[:, None]
    return table.reshape(KZ * GROUP * 2, GROUP * Z)


def z_scale():
    return np.where(np.arange(KZ) == 0, 1.0, 2.0) / float(X * Y * Z)


def tall(table):
    return np.concatenate(split(table), axis=0)


def wide3(table):
    high, low = split(table)
    return np.concatenate([high, low, high], axis=1)


def y_forward():
    return forward_table(Y, KY).reshape(2 * KY, Y * 2)


def x_forward():
    table = forward_table(X, KX).reshape(2 * KX, X // ROWS, ROWS, 2)
    return table.transpose(0, 1, 3, 2).reshape(2 * KX, X * 2)


def nt(left, right):
    return lax.dot_general(left, right, (((1,), (1,)), ((), ())), preferred_element_type=f32)


def tn(left, right):
    return lax.dot_general(left, right, (((0,), (0,)), ((), ())), preferred_element_type=f32)


def nn(left, right):
    return jnp.dot(left, right, preferred_element_type=f32)


def halves(values):
    high = values.astype(bf16)
    low = (values - high.astype(f32)).astype(bf16)
    return high, low


def cells(ref, block):
    return ref[:, :, pl.ds(pl.multiple_of(block * GROUP * Z, GROUP * Z), GROUP * Z)].reshape(
        ROWS * C, GROUP * Z
    )


def z_forward(values, table, q_ref, block):
    half = KZ * GROUP * 2
    both = nt(table, values)
    part = both[:half] + both[half : 2 * half]
    q_ref[:, pl.ds(pl.multiple_of(block * 8, 8), 8), :] = part.reshape(KZ, 8, ROWS * C)
    return both[2 * half :]


def y_to_message(q_ref, dy_ref, o_ref, msg_ref, h):
    table = dy_ref[...]
    span = range(h * KZ // 2, (h + 1) * KZ // 2)
    for kz in span:
        both = nn(table, q_ref[kz].astype(bf16))
        o_ref[kz] = both[: 2 * KY] + both[2 * KY :]
    first, count = chunk_tiles(h)
    for ri in range(2):
        for x in range(ROWS):
            row = jnp.concatenate(
                [o_ref[kz, ri * KY : (ri + 1) * KY, x * C : (x + 1) * C] for kz in span], axis=1
            )
            for t in range(count):
                msg_ref[first + t, pl.ds(ri * ROWS + x, KY, stride=8), :] = row[
                    :, t * LANES : (t + 1) * LANES
                ]


def message_to_y(rb_ref, ey_ref, b_ref, q_ref, h):
    first, count = chunk_tiles(h)
    span = range(h * KZ // 2, (h + 1) * KZ // 2)
    for kz in span if ROWS * C < b_ref.shape[2] else ():
        b_ref[kz, :, ROWS * C :] = jnp.zeros((2 * KY, b_ref.shape[2] - ROWS * C), f32)
    for ri in range(2):
        for x in range(ROWS):
            row = jnp.concatenate(
                [
                    rb_ref[first + t, pl.ds(ri * ROWS + x, KY, stride=8), :]
                    for t in range(count)
                ],
                axis=1,
            )
            for i, kz in enumerate(span):
                b_ref[kz, ri * KY : (ri + 1) * KY, x * C : (x + 1) * C] = row[
                    :, i * C : (i + 1) * C
                ]
    table = ey_ref[...]
    for kz in span:
        high, low = halves(b_ref[kz])
        q_ref[kz] = nn(table, jnp.concatenate([high, high, low], axis=0))


def z_backward(q_ref, table, block):
    part = q_ref[:, pl.ds(pl.multiple_of(block * 8, 8), 8), :]
    part = part.reshape(KZ * 8, q_ref.shape[2])
    turned = part.T[: ROWS * C].astype(bf16)
    return nn(jnp.concatenate([turned, turned], axis=1), table)


def chunk_tiles(h):
    count = KZ * C // LANES // 2
    return h * count, count


def gelu_slope(values):
    size = jnp.abs(values)
    bell = jnp.exp(values * values * -0.5)
    t = 1.0 / (1.0 + (0.3275911 * 0.7071067811865476) * size)
    poly = 0.5 * 1.061405429
    poly = poly * t + 0.5 * -1.453152027
    poly = poly * t + 0.5 * 1.421413741
    poly = poly * t + 0.5 * -0.284496736
    poly = poly * t + 0.5 * 0.254829592
    tail = poly * t * bell
    cumul = jnp.where(values >= 0.0, 1.0 - tail, tail)
    return cumul + values * bell * 0.3989422804014327


def last_kernel(rb_ref, s_ref, wl_ref, ey_ref, bdzs_ref, out_ref, b_ref, q2_ref):
    for h in range(2):
        message_to_y(rb_ref, ey_ref, b_ref, q2_ref, h)
    synth = bdzs_ref[...]
    mixing = wl_ref[...]

    def step(block, carry):
        values = cells(s_ref, block)
        total = z_backward(q2_ref, synth, block) + nn(mixing, values)
        out_ref[:, :, pl.ds(pl.multiple_of(block * GROUP * Z, GROUP * Z), GROUP * Z)] = (
            total.astype(bf16).reshape(ROWS, C, GROUP * Z)
        )
        return carry

    lax.fori_loop(0, Y // GROUP, step, 0, unroll=2)


def others(axis, count, body):
    me = lax.axis_index(axis)

    def step(k, carry):
        body(lax.rem(me + k, count))
        return carry

    lax.fori_loop(1, count, step, 0)


def enter(n, d):
    barrier = pltpu.get_barrier_semaphore()
    for axis, count in (("pencil", n), ("dp", d)):
        others(
            axis,
            count,
            lambda j, axis=axis: pl.semaphore_signal(
                barrier, inc=1, device_id={axis: j}, device_id_type=MESH
            ),
        )
    return barrier


def remote(src, dst, sems, kind, mine, axis, j):
    return pltpu.make_async_remote_copy(
        src_ref=src,
        dst_ref=dst,
        send_sem=sems.at[2 * kind, j],
        recv_sem=sems.at[2 * kind + 1, mine],
        device_id={axis: j},
        device_id_type=MESH,
    )


def wait_one(view, sem):
    pltpu.make_async_copy(view, view, sem).wait()


def arrived(view, sems, kind, axis, count):
    others(axis, count, lambda j: wait_one(view(j), sems.at[2 * kind + 1, j]))


def sent(view, sems, kind, axis, count):
    others(axis, count, lambda j: wait_one(view(j), sems.at[2 * kind, j]))


def piece(ref, h):
    first, count = chunk_tiles(h)
    return lambda j: ref.at[pl.ds(first, count), pl.ds(pl.multiple_of(j * 8, 8), 8), :]


def modes(ref):
    return lambda j: ref.at[pl.ds(pl.multiple_of(j * 2 * KX, 2 * KX), 2 * KX), :]


def swap(src, dst, sems, kind, axis, count):
    me = lax.axis_index(axis)
    others(axis, count, lambda j: remote(src(j), dst(me), sems, kind, me, axis, j).start())


def send_chunk(n, src_ref, dst_ref, sems, kind, h):
    me = lax.axis_index("pencil")
    swap(piece(src_ref, h), piece(dst_ref, h), sems, kind, "pencil", n)
    first, count = chunk_tiles(h)
    mine = pl.ds(pl.multiple_of(me * 8, 8), 8)
    dst_ref[first : first + count, mine, :] = src_ref[first : first + count, mine, :]


def x_analyse(r_ref, dx_ref, g_ref, d, h):
    first, count = chunk_tiles(h)
    high, low = halves(jnp.concatenate([r_ref[first + t] for t in range(count)], axis=1))
    table = dx_ref[...]
    both = nn(table, high)
    spectrum = both[: 2 * KX] + both[2 * KX :] + nn(table[: 2 * KX], low)
    width = KZ * C // d
    for i in range(d // 2):
        j = h * d // 2 + i
        part = spectrum[:, i * width : (i + 1) * width]
        if width < LANES:
            part = jnp.concatenate([part, jnp.zeros((2 * KX, LANES - width), f32)], axis=1)
        g_ref[j * 2 * KX : (j + 1) * 2 * KX, :] = part


def x_synth(h_ref, ex_ref, mb_ref, d, h):
    width = KZ * C // d
    spectrum = jnp.concatenate(
        [
            h_ref[j * 2 * KX : (j + 1) * 2 * KX, 0:width]
            for j in range(h * d // 2, (h + 1) * d // 2)
        ],
        axis=1,
    )
    high, low = halves(spectrum)
    rows = nn(ex_ref[...], jnp.concatenate([high, high, low], axis=0))
    first, count = chunk_tiles(h)
    for t in range(count):
        mb_ref[first + t] = rows[:, t * LANES : (t + 1) * LANES]


def pick(ref, kx, d):
    real = ref[pl.ds(kx, d, stride=2 * KX), :]
    imag = ref[pl.ds(KX + kx, d, stride=2 * KX), :]
    return real, imag


def stage_weights(w_ref, w5_ref, wc_ref):
    for ri in range(2):
        for kz in range(2):
            for c in range(C):
                part = w_ref[ri, 0, kz, :, c * C : (c + 1) * C]
                parts = [part]
                if kz:
                    parts = [jnp.zeros((KX, C), f32), part]
                rest = LANES - C * len(parts)
                if rest:
                    parts = parts + [jnp.zeros((KX, rest), f32)]
                w5_ref[ri, kz, pl.ds(c, KX, stride=C), :] = jnp.concatenate(parts, axis=1)

    def pack(kx, carry):
        rows = pl.ds(pl.multiple_of(kx * C, 8), C)
        for ri in range(2):
            parts = [w5_ref[ri, 0, rows, :], w5_ref[ri, 1, rows, :]]
            if LANES > 2 * C:
                parts.append(jnp.zeros((LANES - 2 * C, LANES), f32))
            high, low = halves(jnp.concatenate(parts, axis=0))
            wc_ref[kx, 0:LANES, ri * LANES : (ri + 1) * LANES] = high
            wc_ref[kx, LANES : 2 * LANES, ri * LANES : (ri + 1) * LANES] = low
        return carry

    lax.fori_loop(0, KX, pack, 0)


def mix_modes(h_ref, wc_ref, g2_ref, d):
    def mix(kx, carry):
        real, imag = pick(h_ref, kx, d)
        high, low = halves(jnp.concatenate([real, imag], axis=0))
        left = jnp.concatenate(
            [
                jnp.concatenate([high, high], axis=1),
                jnp.concatenate([low, jnp.zeros_like(low)], axis=1),
            ],
            axis=0,
        )
        both = nn(left, wc_ref[kx])
        both = both[: 2 * d] + both[2 * d :]
        g2_ref[pl.ds(kx, d, stride=2 * KX), :] = both[:d, :LANES] - both[d:, LANES:]
        g2_ref[pl.ds(KX + kx, d, stride=2 * KX), :] = both[:d, LANES:] + both[d:, :LANES]
        return carry

    lax.fori_loop(0, KX, mix, 0, unroll=4)


def stacked(h_ref, kx, d):
    real, imag = pick(h_ref, kx, d)
    return halves(
        jnp.concatenate(
            [
                jnp.concatenate([real, imag], axis=1),
                jnp.concatenate([imag, -real], axis=1),
            ],
            axis=0,
        )
    )


def adjoint_modes(h_ref, wc_ref, g2_ref, d):
    def adjoint(kx, carry):
        high, low = stacked(h_ref, kx, d)
        both = nt(jnp.concatenate([high, low], axis=0), wc_ref[kx])
        total = both[: 2 * d, :LANES] + both[: 2 * d, LANES:] + both[2 * d :, :LANES]
        g2_ref[pl.ds(kx, d, stride=2 * KX), :] = total[:d]
        g2_ref[pl.ds(KX + kx, d, stride=2 * KX), :] = total[d:]
        return carry

    lax.fori_loop(0, KX, adjoint, 0, unroll=4)


def weight_grad(spec_ref, grad_ref, w5_ref, out_ref, d):
    def one(kx, carry):
        high, low = stacked(grad_ref, kx, d)
        real, imag = pick(spec_ref, kx, d)
        shigh, slow = halves(jnp.concatenate([real, imag], axis=0))
        product = tn(
            jnp.concatenate([shigh, slow, shigh], axis=0),
            jnp.concatenate([high, high, low], axis=0),
        )
        rows = pl.ds(pl.multiple_of(kx * C, 8), C)
        for ri in range(2):
            for kz in range(2):
                w5_ref[ri, kz, rows, :] = product[
                    kz * C : (kz + 1) * C, ri * LANES : (ri + 1) * LANES
                ]
        return carry

    lax.fori_loop(0, KX, one, 0, unroll=2)
    group = 8
    for ri in range(2):
        for kz in range(2):
            for first in range(0, C, group):
                out_ref[ri, 0, kz, :, first * C : (first + group) * C] = jnp.concatenate(
                    [
                        w5_ref[ri, kz, pl.ds(c, KX, stride=C), :][:, kz * C : (kz + 1) * C]
                        for c in range(first, first + group)
                    ],
                    axis=1,
                )


def mode_round(n, d, bufs, tables, psem, dsem, base, between, mixer, extra):
    r_ref, g_ref, h_ref, g2_ref, h2_ref, mb_ref, rb_ref = bufs
    dx_ref, ex_ref = tables
    sample = lax.axis_index("dp")
    half = d // 2
    own = pl.ds(pl.multiple_of(sample * 2 * KX, 2 * KX), 2 * KX)
    between()
    for h in range(2):
        arrived(piece(r_ref, h), psem, base + h, "pencil", n)
        x_analyse(r_ref, dx_ref, g_ref, d, h)

        def to_owner(j, h=h):
            @pl.when(j // half == h)
            def _():
                remote(
                    modes(g_ref)(j), modes(h_ref)(sample), dsem, base // 2, sample, "dp", j
                ).start()

        others("dp", d, to_owner)

        @pl.when(sample // half == h)
        def _():
            h_ref[own, :] = g_ref[own, :]
            arrived(modes(h_ref), dsem, base // 2, "dp", d)
            mixer(h_ref, g2_ref)
            swap(modes(g2_ref), modes(h2_ref), dsem, base // 2 + 1, "dp", d)
            h2_ref[own, :] = g2_ref[own, :]

        if h:
            extra()
    for h in range(2):

        def from_owner(j, h=h):
            @pl.when(j // half == h)
            def _():
                wait_one(modes(h2_ref)(j), dsem.at[2 * (base // 2 + 1) + 1, j])

        others("dp", d, from_owner)
        x_synth(h2_ref, ex_ref, mb_ref, d, h)
        send_chunk(n, mb_ref, rb_ref, psem, base + 2 + h, h)


def main_kernel(
    n, d,
    x_hbm, go_hbm, w_hbm, wl_ref, bdz_ref, bdzs_ref, bdzg_ref, dy_ref, ey_ref, dx_ref, ex_ref,
    s_hbm, rb_out, gs_out, gl_out,
    x_ref, go_ref, s_ref, w_ref, w5_ref, wc_ref, q_ref, q2_ref, o_ref, b_ref, acc_ref,
    msg1_ref, r1_ref, g1_ref, h1_ref, g21_ref, h21_ref, mb1_ref, rb1_ref,
    msg2_ref, r2_ref, g2_ref, h2_ref, g22_ref, h22_ref, mb2_ref, rb2_ref,
    gl_ref, glr_ref, glp_ref, gld_ref, glt_ref, glf_ref,
    psem, dsem, qsem, esem, load_sem,
):
    me, sample = lax.axis_index("pencil"), lax.axis_index("dp")
    tiles = C // 8
    keeper = me < tiles
    blocks = Y // GROUP
    parts = 4
    width = Y * Z // parts
    barrier = enter(n, d)
    loads = []
    for i in range(parts):
        view = (slice(None), slice(None), pl.ds(i * width, width))
        loads.append(
            pltpu.make_async_copy(x_hbm.at[view], x_ref.at[view], load_sem.at[i])
        )
    loads.append(pltpu.make_async_copy(w_hbm, w_ref, load_sem.at[parts]))
    loads.append(pltpu.make_async_copy(go_hbm, go_ref, load_sem.at[parts + 1]))
    for load in loads:
        load.start()
    table = bdz_ref[...]

    def analyse(block, carry):
        z_forward(cells(x_ref, block), table, q_ref, block)
        return carry

    for i in range(parts):
        loads[i].wait()
        lax.fori_loop(i * blocks // parts, (i + 1) * blocks // parts, analyse, 0, unroll=4)
    for h in range(2):
        y_to_message(q_ref, dy_ref, o_ref, msg1_ref, h)
        if h == 0:
            pl.semaphore_wait(barrier, n + d - 2)
        send_chunk(n, msg1_ref, r1_ref, psem, h, h)

    def stage():
        loads[parts].wait()
        stage_weights(w_ref, w5_ref, wc_ref)

    mode_round(
        n, d,
        (r1_ref, g1_ref, h1_ref, g21_ref, h21_ref, mb1_ref, rb1_ref),
        (dx_ref, ex_ref), psem, dsem, 0, stage,
        lambda src, dst: mix_modes(src, wc_ref, dst, d),
        lambda: None,
    )
    acc_ref[...] = jnp.zeros_like(acc_ref)
    loads[parts + 1].wait()
    for h in range(2):
        arrived(piece(rb1_ref, h), psem, 2 + h, "pencil", n)
        message_to_y(rb1_ref, ey_ref, b_ref, q2_ref, h)
    synth = bdzs_ref[...]
    grad_table = bdzg_ref[...]
    mixing = wl_ref[...]

    def slopes(block, carry):
        values = cells(x_ref, block)
        preact = z_backward(q2_ref, synth, block) + nn(mixing, values)
        half = (cells(go_ref, block).astype(f32) * gelu_slope(preact)).astype(bf16)
        s_ref[:, :, pl.ds(pl.multiple_of(block * GROUP * Z, GROUP * Z), GROUP * Z)] = half.reshape(
            ROWS, C, GROUP * Z
        )
        acc_ref[...] += z_forward(
            half, jnp.concatenate([grad_table, values], axis=0), q_ref, block
        )
        return carry

    lax.fori_loop(0, blocks, slopes, 0)
    for h in range(2):
        y_to_message(q_ref, dy_ref, o_ref, msg2_ref, h)
        send_chunk(n, msg2_ref, r2_ref, psem, 4 + h, h)
    store = pltpu.make_async_copy(s_ref, s_hbm, load_sem.at[0])
    store.start()

    def local_sum():
        gl_ref[...] = jnp.zeros_like(gl_ref)
        total = acc_ref[0:C, 0:C]
        for x in range(1, ROWS):
            total = total + acc_ref[x * C : (x + 1) * C, x * C : (x + 1) * C]
        gl_ref[:, :, 0:C] = total.reshape(tiles, 8, C)

        def to_keeper(j):
            @pl.when(j < tiles)
            def _():
                remote(gl_ref.at[j], glr_ref.at[me], qsem, 0, me, "pencil", j).start()

        others("pencil", n, to_keeper)

        @pl.when(keeper)
        def _():
            glr_ref[me] = gl_ref[me]
            arrived(lambda j: glr_ref.at[j], qsem, 0, "pencil", n)
            glp_ref[...] = jnp.sum(glr_ref[...], axis=0)
            others(
                "dp",
                d,
                lambda j: remote(glp_ref, gld_ref.at[sample], esem, 0, sample, "dp", j).start(),
            )
            gld_ref[sample] = glp_ref[...]

    def local_spread():
        @pl.when(keeper)
        def _():
            arrived(lambda j: gld_ref.at[j], esem, 0, "dp", d)
            glt_ref[...] = jnp.sum(gld_ref[...], axis=0)
            others(
                "pencil",
                n,
                lambda j: remote(glt_ref, glf_ref.at[me], qsem, 1, me, "pencil", j).start(),
            )
            glf_ref[me] = glt_ref[...]

    mode_round(
        n, d,
        (r2_ref, g2_ref, h2_ref, g22_ref, h22_ref, mb2_ref, rb2_ref),
        (dx_ref, ex_ref), psem, dsem, 4, local_sum,
        lambda src, dst: adjoint_modes(src, wc_ref, dst, d),
        local_spread,
    )
    weight_grad(h1_ref, h2_ref, w5_ref, gs_out, d)
    for base, (first, modes1, modes2, second) in (
        (0, (msg1_ref, g1_ref, g21_ref, mb1_ref)),
        (4, (msg2_ref, g2_ref, g22_ref, mb2_ref)),
    ):
        for h in range(2):
            sent(piece(first, h), psem, base + h, "pencil", n)
            sent(piece(second, h), psem, base + 2 + h, "pencil", n)
        sent(modes(modes1), dsem, base // 2, "dp", d)
        sent(modes(modes2), dsem, base // 2 + 1, "dp", d)

    def keeper_sent(j):
        @pl.when(j < tiles)
        def _():
            wait_one(gl_ref.at[j], qsem.at[0, j])
            wait_one(glf_ref.at[j], qsem.at[3, j])

    others("pencil", n, keeper_sent)
    gl_out[...] = glf_ref[...]

    @pl.when(keeper)
    def _():
        sent(lambda j: glp_ref, esem, 0, "dp", d)
        sent(lambda j: glt_ref, qsem, 1, "pencil", n)

    store.wait()
    for h in range(2):
        arrived(piece(rb2_ref, h), psem, 6 + h, "pencil", n)
    rb_out[...] = rb2_ref[...]


def call(body, shapes, scratch, arguments, name, places=None, outs=None, collective=None):
    extra = {}
    if collective is not None:
        extra = {"collective_id": collective, "has_side_effects": True}
    vmem = pl.BlockSpec(memory_space=pltpu.VMEM)
    return pl.pallas_call(
        body,
        out_shape=shapes,
        in_specs=places or [vmem] * len(arguments),
        out_specs=outs or jax.tree.map(lambda _: vmem, shapes),
        scratch_shapes=scratch,
        compiler_params=pltpu.CompilerParams(vmem_limit_bytes=LIMIT, **extra),
        cost_estimate=pl.CostEstimate(
            flops=1_000_000_000, bytes_accessed=4_000_000, transcendentals=0
        ),
        name=name,
    )(*arguments)


def local(n, d, field_in, grad_out, w_spec, w_local):
    sds = jax.ShapeDtypeStruct
    lane_tiles = KZ * C // LANES
    values, upstream = field_in[0], grad_out[0]
    cells_shape = values.shape
    ones = np.ones((KZ,))
    scale = z_scale()
    bdz = tall(z_table(ones))
    bdz_grad = tall(z_table(scale))
    synth = tall(z_table(scale))
    synth_plain = tall(z_table(ones))
    dy = tall(y_forward())
    ey = wide3(y_forward().T)
    dx = tall(x_forward())
    ex = wide3(x_forward().T)
    eye = jnp.eye(ROWS, dtype=bf16)
    mixing_back = jnp.kron(eye, w_local)
    mixing = jnp.kron(eye, w_local.T)

    message = sds((lane_tiles, n * 8, LANES), f32)
    q_shape = pltpu.VMEM((KZ, Y * 2, ROWS * C), f32)
    q2_shape = pltpu.VMEM((KZ, Y * 2, 2 * LANES), f32)
    o_shape = pltpu.VMEM((KZ, 2 * KY, ROWS * C), f32)
    b_shape = pltpu.VMEM((KZ, 2 * KY, 2 * LANES), f32)
    mode_shape = pltpu.VMEM((d * 2 * KX, LANES), f32)
    message_shape = pltpu.VMEM((lane_tiles, n * 8, LANES), f32)
    exchange = [message_shape] * 2 + [mode_shape] * 4 + [message_shape] * 2
    tile = pltpu.VMEM((8, LANES), f32)
    tile_count = C // 8
    anywhere = pl.BlockSpec(memory_space=pl.ANY)
    vmem = pl.BlockSpec(memory_space=pltpu.VMEM)
    slopes, rb, grad_spec, grad_local = call(
        functools.partial(main_kernel, n, d),
        (
            sds(cells_shape, bf16),
            message,
            sds(w_spec.shape, f32),
            sds((tile_count, 8, LANES), f32),
        ),
        [
            pltpu.VMEM(cells_shape, bf16),
            pltpu.VMEM(cells_shape, bf16),
            pltpu.VMEM(cells_shape, bf16),
            pltpu.VMEM(w_spec.shape, f32),
            pltpu.VMEM((2, 2, KX * C, LANES), f32),
            pltpu.VMEM((KX, 2 * LANES, 2 * LANES), bf16),
            q_shape,
            q2_shape,
            o_shape,
            b_shape,
            pltpu.VMEM((ROWS * C, ROWS * C), f32),
        ]
        + exchange * 2
        + [
            pltpu.VMEM((tile_count, 8, LANES), f32),
            pltpu.VMEM((n, 8, LANES), f32),
            tile,
            pltpu.VMEM((d, 8, LANES), f32),
            tile,
            pltpu.VMEM((tile_count, 8, LANES), f32),
            pltpu.SemaphoreType.DMA((16, n)),
            pltpu.SemaphoreType.DMA((8, d)),
            pltpu.SemaphoreType.DMA((4, n)),
            pltpu.SemaphoreType.DMA((2, d)),
            pltpu.SemaphoreType.DMA((6,)),
        ],
        (values, upstream, w_spec, mixing, bdz, synth, bdz_grad, dy, ey, dx, ex),
        "spectral_backward",
        places=[anywhere] * 3 + [vmem] * 8,
        outs=(anywhere, vmem, vmem, vmem),
        collective=0,
    )
    grad_in = call(
        last_kernel,
        sds(cells_shape, bf16),
        [b_shape, q2_shape],
        (rb, slopes, mixing_back, ey, synth_plain),
        "plane_synthesis",
    )
    return grad_in[None], grad_spec, grad_local.reshape(C, LANES)[:, :C]


def solution(mesh):
    n, d = mesh.shape["pencil"], mesh.shape["dp"]
    placed = (
        P("dp", "pencil", None, None),
        P("dp", "pencil", None, None),
        P(None, "pencil", "dp", None, None),
        P(),
    )
    return jax.shard_map(
        functools.partial(local, n, d),
        mesh=mesh,
        in_specs=placed,
        out_specs=(P("dp", "pencil", None, None), P(None, "pencil", "dp", None, None), P()),
        check_vma=False,
    )
```

time: 204 us -> 170 us (0.83)
  local copies, waits for them, and re-layouts: 22.2 us -> 4 us
  Pallas kernels: 178 us -> 164 us
  other arithmetic: 3.31 us -> 0.93 us
    pallas_call x5 -> x2, Pallas kernels: 178 us -> 164 us  [call(): pl.pallas_call(body, out_shape=shapes, in_specs=places or [vmem] * len(ar...]
    reshape x3 -> x0, local copies, waits for them, and re-layouts: 12.8 us -> none  [the longest x1 7.57 us: stage_weights(): return both.transpose(2, 0, 3, 1, 4).reshape(KX, 2 * LANES, 2 * LANES)]
    transpose x1 -> x0, local copies, waits for them, and re-layouts: 6.36 us -> none  [stage_weights(): return both.transpose(2, 0, 3, 1, 4).reshape(KX, 2 * LANES, 2 * LANES)]
where the time goes in v1:
time: 170 us
  Pallas kernels  164 us (96%)
  local copies, waits for them, and re-layouts  4 us (2%)
    pallas_call x2, Pallas kernels, call(): pl.pallas_call(body, out_shape=shapes, in_specs=places or [vmem] * len(ar...  164 us

profile of v1, /device:TPU:1, one launch (start us, length us, event | category | flops | bytes accessed | tf_op | source)
XLA Modules:
  0.0 169.6 jit_solution(18236562690316846220)
XLA Ops:
  0.6 0.8 copy.15
  1.4 0.9 broadcast_multiply_fusion
  2.4 0.8 mul.47.wl_ref
  3.1 0.8 mul.44.wl_ref
  3.9 154.4 %spectral_backward.1 = (bf16[4,48,8192]{2,1,0:T(8,128)(2,1)}, f32[6,256,128]{2,1,0:T(8,128)}, f32[2,1,2,32,2304]{4,3,2,1,0:T(8,128)}, f32[6,8,128]{2,1,0:T(8,128)}) custom-call(bf16[4,48,8192]{2,1,0:T(8,128)(2,1)} %bitcast.7, bf16[4,48,8192]{2,1,0:T(8,128)(2,1)} %bitcast.8, f32[2,1,2,32,2304]{4,3,2,1,0:T(8,128)} %w_hbm.1, bf16[192,192]{1,0:T(8,128)(2,1)} %mul.44.wl_ref, ...), custom_call_target="tpu_custom_call" | custom-call | flops 1000000000 | bytes 4000000 | tf_op jit(solution)/shard_map/spectral_backward/pallas_call | solution.py:611
  158.3 0.0 copy-start
  158.3 0.0 copy-start.1
  158.3 9.6 %plane_synthesis.1 = bf16[4,48,8192]{2,1,0:T(8,128)(2,1)} custom-call(f32[6,256,128]{2,1,0:T(8,128)} %get-tuple-element.7.rb_ref, bf16[4,48,8192]{2,1,0:T(8,128)(2,1)} %get-tuple-element.8.s_ref, bf16[192,192]{1,0:T(8,128)(2,1)} %mul.47.wl_ref, bf16[256,192]{1,0:T(8,128)(2,1)} %constant.15.clone.ey_ref, bf16[256,256]{1,0:T(8,128)(2,1)} %constant.12.clone.bdz_ref.bdzs_ref), custom_call_target="tpu_custom_call" | custom-call | flops 1000000000 | bytes 4000000 | tf_op jit(solution)/shard_map/plane_synthesis/pallas_call | solution.py:611
  167.9 0.0 copy-done
  167.9 1.0 copy.18
  169.0 0.0 copy-done.1
  169.0 0.6 copy.19
  (1 shorter events, 0.0 us)
Async XLA Ops:
  158.3 9.6 %copy-start = (f32[2,1,2,32,2304]{4,3,2,1,0:T(8,128)S(1)}, f32[2,1,2,32,2304]{4,3,2,1,0:T(8,128)}, u32[]{:S(2)}) copy-start(f32[2,1,2,32,2304]{4,3,2,1,0:T(8,128)} %get-tuple-element.17) | copy-start | bytes 3538948
  158.3 10.6 %copy-start.1 = (f32[6,8,128]{2,1,0:T(8,128)S(1)}, f32[6,8,128]{2,1,0:T(8,128)}, u32[]{:S(2)}) copy-start(f32[6,8,128]{2,1,0:T(8,128)} %get-tuple-element.10) | copy-start | bytes 73732

commit v2 on v1

--- a/solution.py
+++ b/solution.py
@@ -48,8 +48,22 @@
     return table.reshape(2 * count, length, 2)
 
 
-def z_table(scale):
-    angles = 2.0 * np.pi * (np.outer(np.arange(KZ), np.arange(Z)) % Z) / Z
+def half_of(sample, d):
+    return (sample // max(d // 4, 1)) % 2
+
+
+def owner_order(d):
+    return sorted(range(d), key=lambda j: (half_of(j, d), j))
+
+
+def kz_order(d):
+    return np.array([2 * j + k for j in owner_order(d) for k in range(2)])
+
+
+def z_table(scale, d):
+    order = kz_order(d)
+    scale = scale[order]
+    angles = 2.0 * np.pi * (np.outer(order, np.arange(Z)) % Z) / Z
     table = np.zeros((KZ, GROUP, 2, GROUP, Z))
     for place in range(GROUP):
         table[:, place, 0, place] = np.cos(angles) * scale[:, None]
@@ -65,6 +79,11 @@
     return np.concatenate(split(table), axis=0)
 
 
+def by_half(table):
+    rows = table.shape[0] // 2
+    return np.stack([tall(table[:rows]), tall(table[rows:])])
+
+
 def wide3(table):
     high, low = split(table)
     return np.concatenate([high, low, high], axis=1)
@@ -103,12 +122,13 @@
     )
 
 
-def z_forward(values, table, q_ref, block):
-    half = KZ * GROUP * 2
+def z_forward(values, table, q_ref, block, h):
+    rows = KZ * GROUP
     both = nt(table, values)
-    part = both[:half] + both[half : 2 * half]
-    q_ref[:, pl.ds(pl.multiple_of(block * 8, 8), 8), :] = part.reshape(KZ, 8, ROWS * C)
-    return both[2 * half :]
+    part = both[:rows] + both[rows:]
+    q_ref[h * KZ // 2 : (h + 1) * KZ // 2, pl.ds(pl.multiple_of(block * 8, 8), 8), :] = (
+        part.reshape(KZ // 2, 8, ROWS * C)
+    )
 
 
 def y_to_message(q_ref, dy_ref, o_ref, msg_ref, h):
@@ -179,21 +199,40 @@
     return cumul + values * bell * 0.3989422804014327
 
 
-def last_kernel(rb_ref, s_ref, wl_ref, ey_ref, bdzs_ref, out_ref, b_ref, q2_ref):
-    for h in range(2):
-        message_to_y(rb_ref, ey_ref, b_ref, q2_ref, h)
+def local_matrix(weights):
+    rows = []
+    for x in range(ROWS):
+        parts = [weights]
+        if x:
+            parts = [jnp.zeros((C, x * C), f32)] + parts
+        if x < ROWS - 1:
+            parts = parts + [jnp.zeros((C, (ROWS - 1 - x) * C), f32)]
+        rows.append(jnp.concatenate(parts, axis=1))
+    return jnp.concatenate(rows, axis=0).astype(bf16)
+
+
+def last_kernel(rb_ref, s_ref, wl_ref, ey_ref, bdzs_ref, out_ref, b_ref, q2_ref, mix_ref):
+    part = pl.program_id(0)
+    blocks = s_ref.shape[2] // (GROUP * Z)
+
+    @pl.when(part == 0)
+    def _():
+        mix_ref[...] = local_matrix(wl_ref[...].astype(f32))
+        for h in range(2):
+            message_to_y(rb_ref, ey_ref, b_ref, q2_ref, h)
+
     synth = bdzs_ref[...]
-    mixing = wl_ref[...]
+    mixing = mix_ref[...]
 
     def step(block, carry):
         values = cells(s_ref, block)
-        total = z_backward(q2_ref, synth, block) + nn(mixing, values)
+        total = z_backward(q2_ref, synth, part * blocks + block) + nn(mixing, values)
         out_ref[:, :, pl.ds(pl.multiple_of(block * GROUP * Z, GROUP * Z), GROUP * Z)] = (
             total.astype(bf16).reshape(ROWS, C, GROUP * Z)
         )
         return carry
 
-    lax.fori_loop(0, Y // GROUP, step, 0, unroll=2)
+    lax.fori_loop(0, blocks, step, 0, unroll=True)
 
 
 def others(axis, count, body):
@@ -272,7 +311,7 @@
     spectrum = both[: 2 * KX] + both[2 * KX :] + nn(table[: 2 * KX], low)
     width = KZ * C // d
     for i in range(d // 2):
-        j = h * d // 2 + i
+        j = owner_order(d)[h * d // 2 + i]
         part = spectrum[:, i * width : (i + 1) * width]
         if width < LANES:
             part = jnp.concatenate([part, jnp.zeros((2 * KX, LANES - width), f32)], axis=1)
@@ -284,7 +323,7 @@
     spectrum = jnp.concatenate(
         [
             h_ref[j * 2 * KX : (j + 1) * 2 * KX, 0:width]
-            for j in range(h * d // 2, (h + 1) * d // 2)
+            for j in owner_order(d)[h * d // 2 : (h + 1) * d // 2]
         ],
         axis=1,
     )
@@ -345,7 +384,7 @@
         g2_ref[pl.ds(KX + kx, d, stride=2 * KX), :] = both[:d, LANES:] + both[d:, :LANES]
         return carry
 
-    lax.fori_loop(0, KX, mix, 0, unroll=4)
+    lax.fori_loop(0, KX, mix, 0, unroll=16)
 
 
 def stacked(h_ref, kx, d):
@@ -370,7 +409,7 @@
         g2_ref[pl.ds(KX + kx, d, stride=2 * KX), :] = total[d:]
         return carry
 
-    lax.fori_loop(0, KX, adjoint, 0, unroll=4)
+    lax.fori_loop(0, KX, adjoint, 0, unroll=16)
 
 
 def weight_grad(spec_ref, grad_ref, w5_ref, out_ref, d):
@@ -390,7 +429,7 @@
                 ]
         return carry
 
-    lax.fori_loop(0, KX, one, 0, unroll=2)
+    lax.fori_loop(0, KX, one, 0, unroll=4)
     group = 8
     for ri in range(2):
         for kz in range(2):
@@ -408,49 +447,54 @@
     r_ref, g_ref, h_ref, g2_ref, h2_ref, mb_ref, rb_ref = bufs
     dx_ref, ex_ref = tables
     sample = lax.axis_index("dp")
-    half = d // 2
+    out, back = base // 2, base // 2 + 1
     own = pl.ds(pl.multiple_of(sample * 2 * KX, 2 * KX), 2 * KX)
-    between()
-    for h in range(2):
+
+    def forward(h):
         arrived(piece(r_ref, h), psem, base + h, "pencil", n)
         x_analyse(r_ref, dx_ref, g_ref, d, h)
 
-        def to_owner(j, h=h):
-            @pl.when(j // half == h)
+        def to_owner(j):
+            @pl.when(half_of(j, d) == h)
             def _():
-                remote(
-                    modes(g_ref)(j), modes(h_ref)(sample), dsem, base // 2, sample, "dp", j
-                ).start()
+                remote(modes(g_ref)(j), modes(h_ref)(sample), dsem, out, sample, "dp", j).start()
 
         others("dp", d, to_owner)
 
-        @pl.when(sample // half == h)
+    def mix(h):
+        @pl.when(half_of(sample, d) == h)
         def _():
             h_ref[own, :] = g_ref[own, :]
-            arrived(modes(h_ref), dsem, base // 2, "dp", d)
+            arrived(modes(h_ref), dsem, out, "dp", d)
             mixer(h_ref, g2_ref)
-            swap(modes(g2_ref), modes(h2_ref), dsem, base // 2 + 1, "dp", d)
+            swap(modes(g2_ref), modes(h2_ref), dsem, back, "dp", d)
             h2_ref[own, :] = g2_ref[own, :]
 
-        if h:
-            extra()
-    for h in range(2):
-
-        def from_owner(j, h=h):
-            @pl.when(j // half == h)
+    def backward(h):
+        def from_owner(j):
+            @pl.when(half_of(j, d) == h)
             def _():
-                wait_one(modes(h2_ref)(j), dsem.at[2 * (base // 2 + 1) + 1, j])
+                wait_one(modes(h2_ref)(j), dsem.at[2 * back + 1, j])
 
         others("dp", d, from_owner)
         x_synth(h2_ref, ex_ref, mb_ref, d, h)
         send_chunk(n, mb_ref, rb_ref, psem, base + 2 + h, h)
+
+    between()
+    forward(0)
+    mix(0)
+    forward(1)
+    extra()
+    backward(0)
+    mix(1)
+    backward(1)
 
 
 def main_kernel(
     n, d,
     x_hbm, go_hbm, w_hbm, wl_ref, bdz_ref, bdzs_ref, bdzg_ref, dy_ref, ey_ref, dx_ref, ex_ref,
     s_hbm, rb_out, gs_out, gl_out,
-    x_ref, go_ref, s_ref, w_ref, w5_ref, wc_ref, q_ref, q2_ref, o_ref, b_ref, acc_ref,
+    x_ref, go_ref, s_ref, w_ref, w5_ref, wc_ref, q_ref, q2_ref, o_ref, b_ref,
     msg1_ref, r1_ref, g1_ref, h1_ref, g21_ref, h21_ref, mb1_ref, rb1_ref,
     msg2_ref, r2_ref, g2_ref, h2_ref, g22_ref, h22_ref, mb2_ref, rb2_ref,
     gl_ref, glr_ref, glp_ref, gld_ref, glt_ref, glf_ref,
@@ -473,16 +517,20 @@
     loads.append(pltpu.make_async_copy(go_hbm, go_ref, load_sem.at[parts + 1]))
     for load in loads:
         load.start()
-    table = bdz_ref[...]
-
-    def analyse(block, carry):
-        z_forward(cells(x_ref, block), table, q_ref, block)
-        return carry
-
-    for i in range(parts):
-        loads[i].wait()
-        lax.fori_loop(i * blocks // parts, (i + 1) * blocks // parts, analyse, 0, unroll=4)
+    mixing = local_matrix(wl_ref[...].astype(f32).T)
+
+    def analyse(values_ref, table_ref, h, first, last):
+        def one(block, carry):
+            z_forward(cells(values_ref, block), table_ref[h], q_ref, block, h)
+            return carry
+
+        lax.fori_loop(first, last, one, 0, unroll=8)
+
     for h in range(2):
+        for i in range(parts):
+            if h == 0:
+                loads[i].wait()
+            analyse(x_ref, bdz_ref, h, i * blocks // parts, (i + 1) * blocks // parts)
         y_to_message(q_ref, dy_ref, o_ref, msg1_ref, h)
         if h == 0:
             pl.semaphore_wait(barrier, n + d - 2)
@@ -499,14 +547,11 @@
         lambda src, dst: mix_modes(src, wc_ref, dst, d),
         lambda: None,
     )
-    acc_ref[...] = jnp.zeros_like(acc_ref)
     loads[parts + 1].wait()
     for h in range(2):
         arrived(piece(rb1_ref, h), psem, 2 + h, "pencil", n)
         message_to_y(rb1_ref, ey_ref, b_ref, q2_ref, h)
     synth = bdzs_ref[...]
-    grad_table = bdzg_ref[...]
-    mixing = wl_ref[...]
 
     def slopes(block, carry):
         values = cells(x_ref, block)
@@ -515,13 +560,11 @@
         s_ref[:, :, pl.ds(pl.multiple_of(block * GROUP * Z, GROUP * Z), GROUP * Z)] = half.reshape(
             ROWS, C, GROUP * Z
         )
-        acc_ref[...] += z_forward(
-            half, jnp.concatenate([grad_table, values], axis=0), q_ref, block
-        )
         return carry
 
-    lax.fori_loop(0, blocks, slopes, 0)
+    lax.fori_loop(0, blocks, slopes, 0, unroll=4)
     for h in range(2):
+        analyse(s_ref, bdzg_ref, h, 0, blocks)
         y_to_message(q_ref, dy_ref, o_ref, msg2_ref, h)
         send_chunk(n, msg2_ref, r2_ref, psem, 4 + h, h)
     store = pltpu.make_async_copy(s_ref, s_hbm, load_sem.at[0])
@@ -529,9 +572,9 @@
 
     def local_sum():
         gl_ref[...] = jnp.zeros_like(gl_ref)
-        total = acc_ref[0:C, 0:C]
+        total = nt(x_ref[0], s_ref[0])
         for x in range(1, ROWS):
-            total = total + acc_ref[x * C : (x + 1) * C, x * C : (x + 1) * C]
+            total = total + nt(x_ref[x], s_ref[x])
         gl_ref[:, :, 0:C] = total.reshape(tiles, 8, C)
 
         def to_keeper(j):
@@ -590,7 +633,7 @@
             wait_one(glf_ref.at[j], qsem.at[3, j])
 
     others("pencil", n, keeper_sent)
-    gl_out[...] = glf_ref[...]
+    gl_out[...] = glf_ref[...].reshape(C, LANES)[:, :C]
 
     @pl.when(keeper)
     def _():
@@ -603,23 +646,13 @@
     rb_out[...] = rb2_ref[...]
 
 
-def call(body, shapes, scratch, arguments, name, places=None, outs=None, collective=None):
-    extra = {}
-    if collective is not None:
-        extra = {"collective_id": collective, "has_side_effects": True}
-    vmem = pl.BlockSpec(memory_space=pltpu.VMEM)
-    return pl.pallas_call(
-        body,
-        out_shape=shapes,
-        in_specs=places or [vmem] * len(arguments),
-        out_specs=outs or jax.tree.map(lambda _: vmem, shapes),
-        scratch_shapes=scratch,
-        compiler_params=pltpu.CompilerParams(vmem_limit_bytes=LIMIT, **extra),
-        cost_estimate=pl.CostEstimate(
+def params(**extra):
+    return {
+        "compiler_params": pltpu.CompilerParams(vmem_limit_bytes=LIMIT, **extra),
+        "cost_estimate": pl.CostEstimate(
             flops=1_000_000_000, bytes_accessed=4_000_000, transcendentals=0
         ),
-        name=name,
-    )(*arguments)
+    }
 
 
 def local(n, d, field_in, grad_out, w_spec, w_local):
@@ -629,17 +662,14 @@
     cells_shape = values.shape
     ones = np.ones((KZ,))
     scale = z_scale()
-    bdz = tall(z_table(ones))
-    bdz_grad = tall(z_table(scale))
-    synth = tall(z_table(scale))
-    synth_plain = tall(z_table(ones))
+    bdz = by_half(z_table(ones, d))
+    bdz_grad = by_half(z_table(scale, d))
+    synth = tall(z_table(scale, d))
+    synth_plain = tall(z_table(ones, d))
     dy = tall(y_forward())
     ey = wide3(y_forward().T)
     dx = tall(x_forward())
     ex = wide3(x_forward().T)
-    eye = jnp.eye(ROWS, dtype=bf16)
-    mixing_back = jnp.kron(eye, w_local)
-    mixing = jnp.kron(eye, w_local.T)
 
     message = sds((lane_tiles, n * 8, LANES), f32)
     q_shape = pltpu.VMEM((KZ, Y * 2, ROWS * C), f32)
@@ -653,15 +683,17 @@
     tile_count = C // 8
     anywhere = pl.BlockSpec(memory_space=pl.ANY)
     vmem = pl.BlockSpec(memory_space=pltpu.VMEM)
-    slopes, rb, grad_spec, grad_local = call(
+    slopes, rb, grad_spec, grad_local = pl.pallas_call(
         functools.partial(main_kernel, n, d),
-        (
+        out_shape=(
             sds(cells_shape, bf16),
             message,
             sds(w_spec.shape, f32),
-            sds((tile_count, 8, LANES), f32),
+            sds((C, C), f32),
         ),
-        [
+        in_specs=[anywhere] * 3 + [vmem] * 8,
+        out_specs=(anywhere, vmem, vmem, vmem),
+        scratch_shapes=[
             pltpu.VMEM(cells_shape, bf16),
             pltpu.VMEM(cells_shape, bf16),
             pltpu.VMEM(cells_shape, bf16),
@@ -672,7 +704,6 @@
             q2_shape,
             o_shape,
             b_shape,
-            pltpu.VMEM((ROWS * C, ROWS * C), f32),
         ]
         + exchange * 2
         + [
@@ -688,20 +719,23 @@
             pltpu.SemaphoreType.DMA((2, d)),
             pltpu.SemaphoreType.DMA((6,)),
         ],
-        (values, upstream, w_spec, mixing, bdz, synth, bdz_grad, dy, ey, dx, ex),
-        "spectral_backward",
-        places=[anywhere] * 3 + [vmem] * 8,
-        outs=(anywhere, vmem, vmem, vmem),
-        collective=0,
-    )
-    grad_in = call(
+        name="spectral_backward",
+        **params(collective_id=0, has_side_effects=True),
+    )(values, upstream, w_spec, w_local, bdz, synth, bdz_grad, dy, ey, dx, ex)
+    parts = 4
+    strip = pl.BlockSpec((ROWS, C, Y * Z // parts), lambda i: (0, 0, i))
+    whole = pl.BlockSpec(memory_space=pltpu.VMEM)
+    grad_in = pl.pallas_call(
         last_kernel,
-        sds(cells_shape, bf16),
-        [b_shape, q2_shape],
-        (rb, slopes, mixing_back, ey, synth_plain),
-        "plane_synthesis",
-    )
-    return grad_in[None], grad_spec, grad_local.reshape(C, LANES)[:, :C]
+        out_shape=sds(cells_shape, bf16),
+        grid=(parts,),
+        in_specs=[whole, strip, whole, whole, whole],
+        out_specs=strip,
+        scratch_shapes=[b_shape, q2_shape, pltpu.VMEM((ROWS * C, ROWS * C), bf16)],
+        name="plane_synthesis",
+        **params(),
+    )(rb, slopes, w_local, ey, synth_plain)
+    return grad_in[None], grad_spec, grad_local
 
 
 def solution(mesh):

time: 170 us -> 141 us (0.83)
  Pallas kernels: 164 us -> 138 us
  local copies, waits for them, and re-layouts: 4 us -> 1.63 us
    pallas_call x2, Pallas kernels: 164 us -> 138 us  [the longest x1 131 us: local(): pl.pallas_call(functools.partial(main_kernel, n, d), out_shape=(sds(cells...]
where the time goes in v2:
time: 141 us; the launch traced here: 140 us
  Pallas kernels  138 us (98%)
  local copies, waits for them, and re-layouts  1.63 us (1%)
    pallas_call x1, Pallas kernels, local(): pl.pallas_call(functools.partial(main_kernel, n, d), out_shape=(sds(cells...  131 us
    pallas_call x1, Pallas kernels, local(): pl.pallas_call(last_kernel, out_shape=sds(cells_shape, bf16), grid=(parts...  6.78 us

profile of v2, /device:TPU:1, one launch (start us, length us, event | category | flops | bytes accessed | tf_op | source)
XLA Modules:
  0.0 140.4 jit_solution(3604182181924016469)
XLA Ops:
  0.6 131.3 %spectral_backward.1 = (bf16[4,48,8192]{2,1,0:T(8,128)(2,1)}, f32[6,256,128]{2,1,0:T(8,128)}, f32[2,1,2,32,2304]{4,3,2,1,0:T(8,128)}, f32[48,48]{1,0:T(8,128)}) custom-call(bf16[4,48,8192]{2,1,0:T(8,128)(2,1)} %bitcast.3, bf16[4,48,8192]{2,1,0:T(8,128)(2,1)} %bitcast.4, f32[2,1,2,32,2304]{4,3,2,1,0:T(8,128)} %w_hbm.1, bf16[48,48]{1,0:T(8,128)(2,1)} %wl_ref.3, ...), custom_call_target="tpu_custom_call" | custom-call | flops 1000000000 | bytes 4000000 | tf_op jit(solution)/shard_map/spectral_backward/pallas_call | solution.py:686
  131.9 0.0 copy-start
  131.9 0.0 copy-start.1
  132.0 6.8 %plane_synthesis.1 = bf16[4,48,8192]{2,1,0:T(8,128)(2,1)} custom-call(f32[6,256,128]{2,1,0:T(8,128)} %get-tuple-element.7.rb_ref, bf16[4,48,8192]{2,1,0:T(8,128)(2,1)} %get-tuple-element.8.s_ref, bf16[48,48]{1,0:T(8,128)(2,1)} %wl_ref.3, bf16[256,192]{1,0:T(8,128)(2,1)} %constant.20.clone.ey_ref, bf16[256,256]{1,0:T(8,128)(2,1)} %constant.23.clone.bdzs_ref), custom_call_target="tpu_custom_call" | custom-call | flops 1000000000 | bytes 4000000 | tf_op jit(solution)/shard_map/plane_synthesis/pallas_call | solution.py:728
  138.7 0.0 copy-done
  138.7 1.0 copy.17
  139.8 0.0 copy-done.1
  139.8 0.6 copy.18
Async XLA Ops:
  131.9 6.8 %copy-start = (f32[2,1,2,32,2304]{4,3,2,1,0:T(8,128)S(1)}, f32[2,1,2,32,2304]{4,3,2,1,0:T(8,128)}, u32[]{:S(2)}) copy-start(f32[2,1,2,32,2304]{4,3,2,1,0:T(8,128)} %get-tuple-element.15) | copy-start | bytes 3538948
  131.9 7.8 %copy-start.1 = (f32[48,48]{1,0:T(8,128)S(1)}, f32[48,48]{1,0:T(8,128)}, u32[]{:S(2)}) copy-start(f32[48,48]{1,0:T(8,128)} %get-tuple-element.16) | copy-start | bytes 27652

commit v3 on v2

--- a/solution.py
+++ b/solution.py
@@ -211,12 +211,17 @@
     return jnp.concatenate(rows, axis=0).astype(bf16)
 
 
-def last_kernel(rb_ref, s_ref, wl_ref, ey_ref, bdzs_ref, out_ref, b_ref, q2_ref, mix_ref):
+def last_kernel(
+    rb_ref, s_ref, wl_ref, ey_ref, bdzs_ref, gs_ref, gl_ref,
+    out_ref, gs_out, gl_out, b_ref, q2_ref, mix_ref,
+):
     part = pl.program_id(0)
+    gs_out[...] = gs_ref[...]
     blocks = s_ref.shape[2] // (GROUP * Z)
 
     @pl.when(part == 0)
     def _():
+        gl_out[...] = gl_ref[...]
         mix_ref[...] = local_matrix(wl_ref[...].astype(f32))
         for h in range(2):
             message_to_y(rb_ref, ey_ref, b_ref, q2_ref, h)
@@ -584,6 +589,7 @@
 
         others("pencil", n, to_keeper)
 
+    def local_reduce():
         @pl.when(keeper)
         def _():
             glr_ref[me] = gl_ref[me]
@@ -613,8 +619,9 @@
         (r2_ref, g2_ref, h2_ref, g22_ref, h22_ref, mb2_ref, rb2_ref),
         (dx_ref, ex_ref), psem, dsem, 4, local_sum,
         lambda src, dst: adjoint_modes(src, wc_ref, dst, d),
-        local_spread,
-    )
+        local_reduce,
+    )
+    local_spread()
     weight_grad(h1_ref, h2_ref, w5_ref, gs_out, d)
     for base, (first, modes1, modes2, second) in (
         (0, (msg1_ref, g1_ref, g21_ref, mb1_ref)),
@@ -725,16 +732,19 @@
     parts = 4
     strip = pl.BlockSpec((ROWS, C, Y * Z // parts), lambda i: (0, 0, i))
     whole = pl.BlockSpec(memory_space=pltpu.VMEM)
-    grad_in = pl.pallas_call(
+    modes_strip = pl.BlockSpec(
+        w_spec.shape[:3] + (KX // parts, C * C), lambda i: (0, 0, 0, i, 0)
+    )
+    grad_in, grad_spec, grad_local = pl.pallas_call(
         last_kernel,
-        out_shape=sds(cells_shape, bf16),
+        out_shape=(sds(cells_shape, bf16), sds(w_spec.shape, f32), sds((C, C), f32)),
         grid=(parts,),
-        in_specs=[whole, strip, whole, whole, whole],
-        out_specs=strip,
+        in_specs=[whole, strip, whole, whole, whole, modes_strip, whole],
+        out_specs=(strip, modes_strip, whole),
         scratch_shapes=[b_shape, q2_shape, pltpu.VMEM((ROWS * C, ROWS * C), bf16)],
         name="plane_synthesis",
         **params(),
-    )(rb, slopes, w_local, ey, synth_plain)
+    )(rb, slopes, w_local, ey, synth_plain, grad_spec, grad_local)
     return grad_in[None], grad_spec, grad_local
 
 

time: 141 us -> 135 us (0.957)
  Pallas kernels: 138 us -> 132 us
  local copies, waits for them, and re-layouts: 1.63 us -> 0 us
    pallas_call x1, Pallas kernels: 131 us -> 125 us  [local(): pl.pallas_call(functools.partial(main_kernel, n, d), out_shape=(sds(cells...]
    unnamed x6 -> x0, local copies, waits for them, and re-layouts: 1.63 us -> none
where the time goes in v3:
time: 135 us; the launch traced here: 133 us
  Pallas kernels  132 us (98%)
    pallas_call x1, Pallas kernels, local(): pl.pallas_call(functools.partial(main_kernel, n, d), out_shape=(sds(cells...  125 us
    pallas_call x1, Pallas kernels, local(): pl.pallas_call(last_kernel, out_shape=(sds(cells_shape, bf16), sds(w_spec...  7.17 us

profile of v3, /device:TPU:1, one launch (start us, length us, event | category | flops | bytes accessed | tf_op | source)
XLA Modules:
  0.0 133.1 jit_solution(8632579348710455743)
XLA Ops:
  0.6 125.3 %spectral_backward.1 = (bf16[4,48,8192]{2,1,0:T(8,128)(2,1)}, f32[6,256,128]{2,1,0:T(8,128)}, f32[2,1,2,32,2304]{4,3,2,1,0:T(8,128)}, f32[48,48]{1,0:T(8,128)}) custom-call(bf16[4,48,8192]{2,1,0:T(8,128)(2,1)} %bitcast.3, bf16[4,48,8192]{2,1,0:T(8,128)(2,1)} %bitcast.4, f32[2,1,2,32,2304]{4,3,2,1,0:T(8,128)} %w_hbm.1, bf16[48,48]{1,0:T(8,128)(2,1)} %wl_ref.3, ...), custom_call_target="tpu_custom_call" | custom-call | flops 1000000000 | bytes 4000000 | tf_op jit(solution)/shard_map/spectral_backward/pallas_call | solution.py:693
  125.9 7.2 %plane_synthesis.1 = (bf16[4,48,8192]{2,1,0:T(8,128)(2,1)}, f32[2,1,2,32,2304]{4,3,2,1,0:T(8,128)}, f32[48,48]{1,0:T(8,128)}) custom-call(f32[6,256,128]{2,1,0:T(8,128)} %get-tuple-element.10.rb_ref, bf16[4,48,8192]{2,1,0:T(8,128)(2,1)} %get-tuple-element.11.s_ref, bf16[48,48]{1,0:T(8,128)(2,1)} %wl_ref.3, bf16[256,192]{1,0:T(8,128)(2,1)} %constant.20.clone.ey_ref, ...), custom_call_target="tpu_custom_call" | custom-call | flops 1000000000 | bytes 4000000 | tf_op jit(solution)/shard_map/plane_synthesis/pallas_call | solution.py:738

commit v4 on v2

--- a/solution.py
+++ b/solution.py
@@ -173,11 +173,12 @@
         q_ref[kz] = nn(table, jnp.concatenate([high, high, low], axis=0))
 
 
-def z_backward(q_ref, table, block):
-    part = q_ref[:, pl.ds(pl.multiple_of(block * 8, 8), 8), :]
-    part = part.reshape(KZ * 8, q_ref.shape[2])
+def z_backward(q_ref, table_ref, block, h):
+    rows = pl.ds(pl.multiple_of(block * 8, 8), 8)
+    part = q_ref[h * KZ // 2 : (h + 1) * KZ // 2, rows, :]
+    part = part.reshape(KZ * 4, q_ref.shape[2])
     turned = part.T[: ROWS * C].astype(bf16)
-    return nn(jnp.concatenate([turned, turned], axis=1), table)
+    return nn(jnp.concatenate([turned, turned], axis=1), table_ref[h])
 
 
 def chunk_tiles(h):
@@ -209,30 +210,6 @@
             parts = parts + [jnp.zeros((C, (ROWS - 1 - x) * C), f32)]
         rows.append(jnp.concatenate(parts, axis=1))
     return jnp.concatenate(rows, axis=0).astype(bf16)
-
-
-def last_kernel(rb_ref, s_ref, wl_ref, ey_ref, bdzs_ref, out_ref, b_ref, q2_ref, mix_ref):
-    part = pl.program_id(0)
-    blocks = s_ref.shape[2] // (GROUP * Z)
-
-    @pl.when(part == 0)
-    def _():
-        mix_ref[...] = local_matrix(wl_ref[...].astype(f32))
-        for h in range(2):
-            message_to_y(rb_ref, ey_ref, b_ref, q2_ref, h)
-
-    synth = bdzs_ref[...]
-    mixing = mix_ref[...]
-
-    def step(block, carry):
-        values = cells(s_ref, block)
-        total = z_backward(q2_ref, synth, part * blocks + block) + nn(mixing, values)
-        out_ref[:, :, pl.ds(pl.multiple_of(block * GROUP * Z, GROUP * Z), GROUP * Z)] = (
-            total.astype(bf16).reshape(ROWS, C, GROUP * Z)
-        )
-        return carry
-
-    lax.fori_loop(0, blocks, step, 0, unroll=True)
 
 
 def others(axis, count, body):
@@ -492,9 +469,9 @@
 
 def main_kernel(
     n, d,
-    x_hbm, go_hbm, w_hbm, wl_ref, bdz_ref, bdzs_ref, bdzg_ref, dy_ref, ey_ref, dx_ref, ex_ref,
-    s_hbm, rb_out, gs_out, gl_out,
-    x_ref, go_ref, s_ref, w_ref, w5_ref, wc_ref, q_ref, q2_ref, o_ref, b_ref,
+    x_hbm, go_hbm, w_hbm, wl_ref, bdz_ref, bdzg_ref, dy_ref, ey_ref, dx_ref, ex_ref,
+    out_ref, gs_out, gl_out,
+    x_ref, go_ref, s_ref, p_ref, w_ref, w5_ref, wc_ref, q_ref, q2_ref, o_ref, b_ref,
     msg1_ref, r1_ref, g1_ref, h1_ref, g21_ref, h21_ref, mb1_ref, rb1_ref,
     msg2_ref, r2_ref, g2_ref, h2_ref, g22_ref, h22_ref, mb2_ref, rb2_ref,
     gl_ref, glr_ref, glp_ref, gld_ref, glt_ref, glf_ref,
@@ -517,7 +494,8 @@
     loads.append(pltpu.make_async_copy(go_hbm, go_ref, load_sem.at[parts + 1]))
     for load in loads:
         load.start()
-    mixing = local_matrix(wl_ref[...].astype(f32).T)
+    weights = wl_ref[...].astype(f32)
+    mixing = local_matrix(weights.T)
 
     def analyse(values_ref, table_ref, h, first, last):
         def one(block, carry):
@@ -548,27 +526,36 @@
         lambda: None,
     )
     loads[parts + 1].wait()
-    for h in range(2):
-        arrived(piece(rb1_ref, h), psem, 2 + h, "pencil", n)
-        message_to_y(rb1_ref, ey_ref, b_ref, q2_ref, h)
-    synth = bdzs_ref[...]
-
-    def slopes(block, carry):
-        values = cells(x_ref, block)
-        preact = z_backward(q2_ref, synth, block) + nn(mixing, values)
+
+    def strip(block):
+        return pl.ds(pl.multiple_of(block * GROUP * Z, GROUP * Z), GROUP * Z)
+
+    def synthesize(rb_ref, kind, table_ref, matrix, values_ref, finish):
+        def begin(block, carry):
+            p_ref[:, strip(block)] = z_backward(q2_ref, table_ref, block, 0) + nn(
+                matrix, cells(values_ref, block)
+            )
+            return carry
+
+        def end(block, carry):
+            total = p_ref[:, strip(block)] + z_backward(q2_ref, table_ref, block, 1)
+            finish(block, total)
+            return carry
+
+        for h, loop in enumerate((begin, end)):
+            arrived(piece(rb_ref, h), psem, kind + h, "pencil", n)
+            message_to_y(rb_ref, ey_ref, b_ref, q2_ref, h)
+            lax.fori_loop(0, blocks, loop, 0, unroll=4)
+
+    def slopes(block, preact):
         half = (cells(go_ref, block).astype(f32) * gelu_slope(preact)).astype(bf16)
-        s_ref[:, :, pl.ds(pl.multiple_of(block * GROUP * Z, GROUP * Z), GROUP * Z)] = half.reshape(
-            ROWS, C, GROUP * Z
-        )
-        return carry
-
-    lax.fori_loop(0, blocks, slopes, 0, unroll=4)
+        s_ref[:, :, strip(block)] = half.reshape(ROWS, C, GROUP * Z)
+
+    synthesize(rb1_ref, 2, bdzg_ref, mixing, x_ref, slopes)
     for h in range(2):
         analyse(s_ref, bdzg_ref, h, 0, blocks)
         y_to_message(q_ref, dy_ref, o_ref, msg2_ref, h)
         send_chunk(n, msg2_ref, r2_ref, psem, 4 + h, h)
-    store = pltpu.make_async_copy(s_ref, s_hbm, load_sem.at[0])
-    store.start()
 
     def local_sum():
         gl_ref[...] = jnp.zeros_like(gl_ref)
@@ -584,6 +571,7 @@
 
         others("pencil", n, to_keeper)
 
+    def local_reduce():
         @pl.when(keeper)
         def _():
             glr_ref[me] = gl_ref[me]
@@ -613,8 +601,9 @@
         (r2_ref, g2_ref, h2_ref, g22_ref, h22_ref, mb2_ref, rb2_ref),
         (dx_ref, ex_ref), psem, dsem, 4, local_sum,
         lambda src, dst: adjoint_modes(src, wc_ref, dst, d),
-        local_spread,
-    )
+        local_reduce,
+    )
+    local_spread()
     weight_grad(h1_ref, h2_ref, w5_ref, gs_out, d)
     for base, (first, modes1, modes2, second) in (
         (0, (msg1_ref, g1_ref, g21_ref, mb1_ref)),
@@ -640,10 +629,10 @@
         sent(lambda j: glp_ref, esem, 0, "dp", d)
         sent(lambda j: glt_ref, qsem, 1, "pencil", n)
 
-    store.wait()
-    for h in range(2):
-        arrived(piece(rb2_ref, h), psem, 6 + h, "pencil", n)
-    rb_out[...] = rb2_ref[...]
+    def gradient(block, total):
+        out_ref[:, :, strip(block)] = total.astype(bf16).reshape(ROWS, C, GROUP * Z)
+
+    synthesize(rb2_ref, 6, bdz_ref, local_matrix(weights), s_ref, gradient)
 
 
 def params(**extra):
@@ -664,14 +653,11 @@
     scale = z_scale()
     bdz = by_half(z_table(ones, d))
     bdz_grad = by_half(z_table(scale, d))
-    synth = tall(z_table(scale, d))
-    synth_plain = tall(z_table(ones, d))
     dy = tall(y_forward())
     ey = wide3(y_forward().T)
     dx = tall(x_forward())
     ex = wide3(x_forward().T)
 
-    message = sds((lane_tiles, n * 8, LANES), f32)
     q_shape = pltpu.VMEM((KZ, Y * 2, ROWS * C), f32)
     q2_shape = pltpu.VMEM((KZ, Y * 2, 2 * LANES), f32)
     o_shape = pltpu.VMEM((KZ, 2 * KY, ROWS * C), f32)
@@ -683,20 +669,16 @@
     tile_count = C // 8
     anywhere = pl.BlockSpec(memory_space=pl.ANY)
     vmem = pl.BlockSpec(memory_space=pltpu.VMEM)
-    slopes, rb, grad_spec, grad_local = pl.pallas_call(
+    grad_in, grad_spec, grad_local = pl.pallas_call(
         functools.partial(main_kernel, n, d),
-        out_shape=(
-            sds(cells_shape, bf16),
-            message,
-            sds(w_spec.shape, f32),
-            sds((C, C), f32),
-        ),
-        in_specs=[anywhere] * 3 + [vmem] * 8,
-        out_specs=(anywhere, vmem, vmem, vmem),
+        out_shape=(sds(cells_shape, bf16), sds(w_spec.shape, f32), sds((C, C), f32)),
+        in_specs=[anywhere] * 3 + [vmem] * 7,
+        out_specs=(vmem, vmem, vmem),
         scratch_shapes=[
             pltpu.VMEM(cells_shape, bf16),
             pltpu.VMEM(cells_shape, bf16),
             pltpu.VMEM(cells_shape, bf16),
+            pltpu.VMEM((ROWS * C, Y * Z), f32),
             pltpu.VMEM(w_spec.shape, f32),
             pltpu.VMEM((2, 2, KX * C, LANES), f32),
             pltpu.VMEM((KX, 2 * LANES, 2 * LANES), bf16),
@@ -721,20 +703,7 @@
         ],
         name="spectral_backward",
         **params(collective_id=0, has_side_effects=True),
-    )(values, upstream, w_spec, w_local, bdz, synth, bdz_grad, dy, ey, dx, ex)
-    parts = 4
-    strip = pl.BlockSpec((ROWS, C, Y * Z // parts), lambda i: (0, 0, i))
-    whole = pl.BlockSpec(memory_space=pltpu.VMEM)
-    grad_in = pl.pallas_call(
-        last_kernel,
-        out_shape=sds(cells_shape, bf16),
-        grid=(parts,),
-        in_specs=[whole, strip, whole, whole, whole],
-        out_specs=strip,
-        scratch_shapes=[b_shape, q2_shape, pltpu.VMEM((ROWS * C, ROWS * C), bf16)],
-        name="plane_synthesis",
-        **params(),
-    )(rb, slopes, w_local, ey, synth_plain)
+    )(values, upstream, w_spec, w_local, bdz, bdz_grad, dy, ey, dx, ex)
     return grad_in[None], grad_spec, grad_local
 
 

time: 141 us -> 145 us (1.028)
  local copies, waits for them, and re-layouts: 1.63 us -> 5.58 us
    pallas_call x1, Pallas kernels: 131 us -> 139 us  [local(): pl.pallas_call(functools.partial(main_kernel, n, d), out_shape=(sds(cells...]
    pallas_call x1 -> x0, Pallas kernels: 6.78 us -> none  [local(): pl.pallas_call(last_kernel, out_shape=sds(cells_shape, bf16), grid=(parts...]
    unnamed x6 -> x7, local copies, waits for them, and re-layouts: 1.63 us -> 5.58 us
where the time goes in v4:
time: 145 us
  Pallas kernels  139 us (96%)
  local copies, waits for them, and re-layouts  5.58 us (4%)
    pallas_call x1, Pallas kernels, local(): pl.pallas_call(functools.partial(main_kernel, n, d), out_shape=(sds(cells...  139 us
    unnamed x7, local copies, waits for them, and re-layouts  5.58 us

profile of v4, /device:TPU:1, one launch (start us, length us, event | category | flops | bytes accessed | tf_op | source)
XLA Modules:
  0.0 144.8 jit_solution(17714844328251907831)
XLA Ops:
  0.6 138.5 %spectral_backward.1 = (bf16[4,48,8192]{2,1,0:T(8,128)(2,1)}, f32[2,1,2,32,2304]{4,3,2,1,0:T(8,128)}, f32[48,48]{1,0:T(8,128)}) custom-call(bf16[4,48,8192]{2,1,0:T(8,128)(2,1)} %bitcast.3, bf16[4,48,8192]{2,1,0:T(8,128)(2,1)} %bitcast.4, f32[2,1,2,32,2304]{4,3,2,1,0:T(8,128)} %w_hbm.1, bf16[48,48]{1,0:T(8,128)(2,1)} %wl_ref.1, ...), custom_call_target="tpu_custom_call" | custom-call | flops 1000000000 | bytes 4000000 | tf_op jit(solution)/shard_map/spectral_backward/pallas_call | solution.py:672
  139.2 0.0 copy-start
  139.2 0.0 copy-start.1
  139.2 4.0 %copy.16 = bf16[1,4,48,8192]{3,2,1,0:T(8,128)(2,1)} copy(bf16[1,4,48,8192]{3,2,1,0:T(8,128)(2,1)} %bitcast.5) | data formatting | bytes 6291456
  143.1 0.0 copy-done
  143.1 1.0 copy.17
  144.2 0.0 copy-done.1
  144.2 0.6 copy.18
Async XLA Ops:
  139.2 4.0 %copy-start = (f32[2,1,2,32,2304]{4,3,2,1,0:T(8,128)S(1)}, f32[2,1,2,32,2304]{4,3,2,1,0:T(8,128)}, u32[]{:S(2)}) copy-start(f32[2,1,2,32,2304]{4,3,2,1,0:T(8,128)} %get-tuple-element.13) | copy-start | bytes 3538948
  139.2 5.0 %copy-start.1 = (f32[48,48]{1,0:T(8,128)S(1)}, f32[48,48]{1,0:T(8,128)}, u32[]{:S(2)}) copy-start(f32[48,48]{1,0:T(8,128)} %get-tuple-element.14) | copy-start | bytes 27652

commit v5 on v3

--- a/solution.py
+++ b/solution.py
@@ -300,12 +300,34 @@
     others(axis, count, lambda j: remote(src(j), dst(me), sems, kind, me, axis, j).start())
 
 
-def send_chunk(n, src_ref, dst_ref, sems, kind, h):
+def send_chunk(n, src_ref, dst_ref, sems, kind, h, own_sem=None):
     me = lax.axis_index("pencil")
-    swap(piece(src_ref, h), piece(dst_ref, h), sems, kind, "pencil", n)
+    src, dst = piece(src_ref, h), piece(dst_ref, h)
+
+    def send(j):
+        pltpu.make_async_remote_copy(
+            src_ref=src(j),
+            dst_ref=dst(me),
+            send_sem=sems.at[2 * kind],
+            recv_sem=sems.at[2 * kind + 1],
+            device_id={"pencil": j},
+            device_id_type=MESH,
+        ).start()
+
+    others("pencil", n, send)
+    if own_sem is not None:
+        pltpu.make_async_copy(src(me), dst(me), own_sem).start()
+        return
     first, count = chunk_tiles(h)
     mine = pl.ds(pl.multiple_of(me * 8, 8), 8)
     dst_ref[first : first + count, mine, :] = src_ref[first : first + count, mine, :]
+
+
+def planes_wait(n, ref, sems, kind, h, received):
+    first, count = chunk_tiles(h)
+    wait_one(
+        ref.at[pl.ds(first, count), pl.ds(0, (n - 1) * 8), :], sems.at[2 * kind + int(received)]
+    )
 
 
 def x_analyse(r_ref, dx_ref, g_ref, d, h):
@@ -448,7 +470,7 @@
                 )
 
 
-def mode_round(n, d, bufs, tables, psem, dsem, base, between, mixer, extra):
+def mode_round(n, d, bufs, tables, psem, dsem, base, between, mixer, extra, own_sem=None):
     r_ref, g_ref, h_ref, g2_ref, h2_ref, mb_ref, rb_ref = bufs
     dx_ref, ex_ref = tables
     sample = lax.axis_index("dp")
@@ -456,7 +478,7 @@
     own = pl.ds(pl.multiple_of(sample * 2 * KX, 2 * KX), 2 * KX)
 
     def forward(h):
-        arrived(piece(r_ref, h), psem, base + h, "pencil", n)
+        planes_wait(n, r_ref, psem, base + h, h, True)
         x_analyse(r_ref, dx_ref, g_ref, d, h)
 
         def to_owner(j):
@@ -483,7 +505,9 @@
 
         others("dp", d, from_owner)
         x_synth(h2_ref, ex_ref, mb_ref, d, h)
-        send_chunk(n, mb_ref, rb_ref, psem, base + 2 + h, h)
+        send_chunk(
+            n, mb_ref, rb_ref, psem, base + 2 + h, h, None if own_sem is None else own_sem.at[h]
+        )
 
     between()
     forward(0)
@@ -498,10 +522,10 @@
 def main_kernel(
     n, d,
     x_hbm, go_hbm, w_hbm, wl_ref, bdz_ref, bdzs_ref, bdzg_ref, dy_ref, ey_ref, dx_ref, ex_ref,
-    s_hbm, rb_out, gs_out, gl_out,
-    x_ref, go_ref, s_ref, w_ref, w5_ref, wc_ref, q_ref, q2_ref, o_ref, b_ref,
+    s_hbm, rb_hbm, gs_hbm, gl_hbm,
+    x_ref, go_ref, s_ref, p_ref, gs_ref, glo_ref, w_ref, w5_ref, wc_ref, q_ref, q2_ref, o_ref, b_ref,
     msg1_ref, r1_ref, g1_ref, h1_ref, g21_ref, h21_ref, mb1_ref, rb1_ref,
-    msg2_ref, r2_ref, g2_ref, h2_ref, g22_ref, h22_ref, mb2_ref, rb2_ref,
+    msg2_ref, r2_ref, g2_ref, h2_ref, g22_ref, h22_ref, mb2_ref,
     gl_ref, glr_ref, glp_ref, gld_ref, glt_ref, glf_ref,
     psem, dsem, qsem, esem, load_sem,
 ):
@@ -524,6 +548,9 @@
         load.start()
     mixing = local_matrix(wl_ref[...].astype(f32).T)
 
+    def strip(block):
+        return pl.ds(pl.multiple_of(block * GROUP * Z, GROUP * Z), GROUP * Z)
+
     def analyse(values_ref, table_ref, h, first, last):
         def one(block, carry):
             z_forward(cells(values_ref, block), table_ref[h], q_ref, block, h)
@@ -542,6 +569,11 @@
         send_chunk(n, msg1_ref, r1_ref, psem, h, h)
 
     def stage():
+        def product(block, carry):
+            p_ref[:, strip(block)] = nn(mixing, cells(x_ref, block))
+            return carry
+
+        lax.fori_loop(0, blocks, product, 0, unroll=8)
         loads[parts].wait()
         stage_weights(w_ref, w5_ref, wc_ref)
 
@@ -554,20 +586,17 @@
     )
     loads[parts + 1].wait()
     for h in range(2):
-        arrived(piece(rb1_ref, h), psem, 2 + h, "pencil", n)
+        planes_wait(n, rb1_ref, psem, 2 + h, h, True)
         message_to_y(rb1_ref, ey_ref, b_ref, q2_ref, h)
     synth = bdzs_ref[...]
 
     def slopes(block, carry):
-        values = cells(x_ref, block)
-        preact = z_backward(q2_ref, synth, block) + nn(mixing, values)
+        preact = p_ref[:, strip(block)] + z_backward(q2_ref, synth, block)
         half = (cells(go_ref, block).astype(f32) * gelu_slope(preact)).astype(bf16)
-        s_ref[:, :, pl.ds(pl.multiple_of(block * GROUP * Z, GROUP * Z), GROUP * Z)] = half.reshape(
-            ROWS, C, GROUP * Z
-        )
+        s_ref[:, :, strip(block)] = half.reshape(ROWS, C, GROUP * Z)
         return carry
 
-    lax.fori_loop(0, blocks, slopes, 0, unroll=4)
+    lax.fori_loop(0, blocks, slopes, 0, unroll=8)
     for h in range(2):
         analyse(s_ref, bdzg_ref, h, 0, blocks)
         y_to_message(q_ref, dy_ref, o_ref, msg2_ref, h)
@@ -616,20 +645,26 @@
 
     mode_round(
         n, d,
-        (r2_ref, g2_ref, h2_ref, g22_ref, h22_ref, mb2_ref, rb2_ref),
+        (r2_ref, g2_ref, h2_ref, g22_ref, h22_ref, mb2_ref, rb_hbm),
         (dx_ref, ex_ref), psem, dsem, 4, local_sum,
         lambda src, dst: adjoint_modes(src, wc_ref, dst, d),
         local_reduce,
+        load_sem.at[pl.ds(1, 2)],
     )
     local_spread()
-    weight_grad(h1_ref, h2_ref, w5_ref, gs_out, d)
+    weight_grad(h1_ref, h2_ref, w5_ref, gs_ref, d)
+    stores = [
+        pltpu.make_async_copy(gs_ref, gs_hbm, load_sem.at[3]),
+        pltpu.make_async_copy(glo_ref, gl_hbm, load_sem.at[4]),
+    ]
+    stores[0].start()
     for base, (first, modes1, modes2, second) in (
         (0, (msg1_ref, g1_ref, g21_ref, mb1_ref)),
         (4, (msg2_ref, g2_ref, g22_ref, mb2_ref)),
     ):
         for h in range(2):
-            sent(piece(first, h), psem, base + h, "pencil", n)
-            sent(piece(second, h), psem, base + 2 + h, "pencil", n)
+            planes_wait(n, first, psem, base + h, h, False)
+            planes_wait(n, second, psem, base + 2 + h, h, False)
         sent(modes(modes1), dsem, base // 2, "dp", d)
         sent(modes(modes2), dsem, base // 2 + 1, "dp", d)
 
@@ -640,7 +675,8 @@
             wait_one(glf_ref.at[j], qsem.at[3, j])
 
     others("pencil", n, keeper_sent)
-    gl_out[...] = glf_ref[...].reshape(C, LANES)[:, :C]
+    glo_ref[...] = glf_ref[...].reshape(C, LANES)[:, :C]
+    stores[1].start()
 
     @pl.when(keeper)
     def _():
@@ -648,9 +684,12 @@
         sent(lambda j: glt_ref, qsem, 1, "pencil", n)
 
     store.wait()
+    for one in stores:
+        one.wait()
     for h in range(2):
-        arrived(piece(rb2_ref, h), psem, 6 + h, "pencil", n)
-    rb_out[...] = rb2_ref[...]
+        own = piece(mb2_ref, h)(me)
+        pltpu.make_async_copy(own, piece(rb_hbm, h)(me), load_sem.at[1 + h]).wait()
+        planes_wait(n, rb_hbm, psem, 6 + h, h, True)
 
 
 def params(**extra):
@@ -699,11 +738,14 @@
             sds((C, C), f32),
         ),
         in_specs=[anywhere] * 3 + [vmem] * 8,
-        out_specs=(anywhere, vmem, vmem, vmem),
+        out_specs=(anywhere,) * 4,
         scratch_shapes=[
             pltpu.VMEM(cells_shape, bf16),
             pltpu.VMEM(cells_shape, bf16),
             pltpu.VMEM(cells_shape, bf16),
+            pltpu.VMEM((ROWS * C, Y * Z), f32),
+            pltpu.VMEM(w_spec.shape, f32),
+            pltpu.VMEM((C, C), f32),
             pltpu.VMEM(w_spec.shape, f32),
             pltpu.VMEM((2, 2, KX * C, LANES), f32),
             pltpu.VMEM((KX, 2 * LANES, 2 * LANES), bf16),
@@ -712,7 +754,7 @@
             o_shape,
             b_shape,
         ]
-        + exchange * 2
+        + exchange + exchange[:-1]
         + [
             pltpu.VMEM((tile_count, 8, LANES), f32),
             pltpu.VMEM((n, 8, LANES), f32),
@@ -720,7 +762,7 @@
             pltpu.VMEM((d, 8, LANES), f32),
             tile,
             pltpu.VMEM((tile_count, 8, LANES), f32),
-            pltpu.SemaphoreType.DMA((16, n)),
+            pltpu.SemaphoreType.DMA((16,)),
             pltpu.SemaphoreType.DMA((8, d)),
             pltpu.SemaphoreType.DMA((4, n)),
             pltpu.SemaphoreType.DMA((2, d)),

time: 135 us -> 128 us (0.948)
  Pallas kernels: 132 us -> 126 us
    pallas_call x1, Pallas kernels: 125 us -> 119 us  [local(): pl.pallas_call(functools.partial(main_kernel, n, d), out_shape=(sds(cells...]
where the time goes in v5:
time: 128 us; the launch traced here: 127 us
  Pallas kernels  126 us (98%)
    pallas_call x1, Pallas kernels, local(): pl.pallas_call(functools.partial(main_kernel, n, d), out_shape=(sds(cells...  119 us
    pallas_call x1, Pallas kernels, local(): pl.pallas_call(last_kernel, out_shape=(sds(cells_shape, bf16), sds(w_spec...  7.18 us

profile of v5, /device:TPU:1, one launch (start us, length us, event | category | flops | bytes accessed | tf_op | source)
XLA Modules:
  0.0 126.8 jit_solution(16451944144461104526)
XLA Ops:
  0.6 118.9 %spectral_backward.1 = (bf16[4,48,8192]{2,1,0:T(8,128)(2,1)}, f32[6,256,128]{2,1,0:T(8,128)}, f32[2,1,2,32,2304]{4,3,2,1,0:T(8,128)}, f32[48,48]{1,0:T(8,128)}) custom-call(bf16[4,48,8192]{2,1,0:T(8,128)(2,1)} %bitcast.3, bf16[4,48,8192]{2,1,0:T(8,128)(2,1)} %bitcast.4, f32[2,1,2,32,2304]{4,3,2,1,0:T(8,128)} %w_hbm.1, bf16[48,48]{1,0:T(8,128)(2,1)} %wl_ref.3, ...), custom_call_target="tpu_custom_call" | custom-call | flops 1000000000 | bytes 4000000 | tf_op jit(solution)/shard_map/spectral_backward/pallas_call | solution.py:732
  119.6 7.2 %plane_synthesis.1 = (bf16[4,48,8192]{2,1,0:T(8,128)(2,1)}, f32[2,1,2,32,2304]{4,3,2,1,0:T(8,128)}, f32[48,48]{1,0:T(8,128)}) custom-call(f32[6,256,128]{2,1,0:T(8,128)} %get-tuple-element.10.rb_ref, bf16[4,48,8192]{2,1,0:T(8,128)(2,1)} %get-tuple-element.11.s_ref, bf16[48,48]{1,0:T(8,128)(2,1)} %wl_ref.3, bf16[256,192]{1,0:T(8,128)(2,1)} %constant.20.clone.ey_ref, ...), custom_call_target="tpu_custom_call" | custom-call | flops 1000000000 | bytes 4000000 | tf_op jit(solution)/shard_map/plane_synthesis/pallas_call | solution.py:780

commit v6 on v5

--- a/solution.py
+++ b/solution.py
@@ -411,7 +411,7 @@
         g2_ref[pl.ds(KX + kx, d, stride=2 * KX), :] = both[:d, LANES:] + both[d:, :LANES]
         return carry
 
-    lax.fori_loop(0, KX, mix, 0, unroll=16)
+    lax.fori_loop(0, KX, mix, 0, unroll=True)
 
 
 def stacked(h_ref, kx, d):
@@ -436,7 +436,7 @@
         g2_ref[pl.ds(KX + kx, d, stride=2 * KX), :] = total[d:]
         return carry
 
-    lax.fori_loop(0, KX, adjoint, 0, unroll=16)
+    lax.fori_loop(0, KX, adjoint, 0, unroll=True)
 
 
 def weight_grad(spec_ref, grad_ref, w5_ref, out_ref, d):
@@ -771,7 +771,7 @@
         name="spectral_backward",
         **params(collective_id=0, has_side_effects=True),
     )(values, upstream, w_spec, w_local, bdz, synth, bdz_grad, dy, ey, dx, ex)
-    parts = 4
+    parts = 2
     strip = pl.BlockSpec((ROWS, C, Y * Z // parts), lambda i: (0, 0, i))
     whole = pl.BlockSpec(memory_space=pltpu.VMEM)
     modes_strip = pl.BlockSpec(

time: 128 us -> 126 us (0.984)
  no operation moved by 1% of the time
where the time goes in v6:
time: 126 us
  Pallas kernels  125 us (99%)
    pallas_call x1, Pallas kernels, local(): pl.pallas_call(functools.partial(main_kernel, n, d), out_shape=(sds(cells...  118 us
    pallas_call x1, Pallas kernels, local(): pl.pallas_call(last_kernel, out_shape=(sds(cells_shape, bf16), sds(w_spec...  6.43 us

profile of v6, /device:TPU:1, one launch (start us, length us, event | category | flops | bytes accessed | tf_op | source)
XLA Modules:
  0.0 125.5 jit_solution(1229316202360868839)
XLA Ops:
  0.6 118.3 %spectral_backward.1 = (bf16[4,48,8192]{2,1,0:T(8,128)(2,1)}, f32[6,256,128]{2,1,0:T(8,128)}, f32[2,1,2,32,2304]{4,3,2,1,0:T(8,128)}, f32[48,48]{1,0:T(8,128)}) custom-call(bf16[4,48,8192]{2,1,0:T(8,128)(2,1)} %bitcast.3, bf16[4,48,8192]{2,1,0:T(8,128)(2,1)} %bitcast.4, f32[2,1,2,32,2304]{4,3,2,1,0:T(8,128)} %w_hbm.1, bf16[48,48]{1,0:T(8,128)(2,1)} %wl_ref.3, ...), custom_call_target="tpu_custom_call" | custom-call | flops 1000000000 | bytes 4000000 | tf_op jit(solution)/shard_map/spectral_backward/pallas_call | solution.py:732
  118.9 6.4 %plane_synthesis.1 = (bf16[4,48,8192]{2,1,0:T(8,128)(2,1)}, f32[2,1,2,32,2304]{4,3,2,1,0:T(8,128)}, f32[48,48]{1,0:T(8,128)}) custom-call(f32[6,256,128]{2,1,0:T(8,128)} %get-tuple-element.10.rb_ref, bf16[4,48,8192]{2,1,0:T(8,128)(2,1)} %get-tuple-element.11.s_ref, bf16[48,48]{1,0:T(8,128)(2,1)} %wl_ref.3, bf16[256,192]{1,0:T(8,128)(2,1)} %constant.20.clone.ey_ref, ...), custom_call_target="tpu_custom_call" | custom-call | flops 1000000000 | bytes 4000000 | tf_op jit(solution)/shard_map/plane_synthesis/pallas_call | solution.py:780
